TPU v7x, 256 devices: a whole 4x4x8 slice. The times are simulated.
256 devices in a mesh: img: 4 (over x), row: 8 (over z_hi, y), col: 8 (over z_lo, core).
Axes of the slice: x: 4, y: 4, z: 8 (z_hi: 2, z_lo: 4; z = z_hi * 4 + z_lo), core: 2. Of those that a mesh axis runs over, the one named last changes fastest.
Arguments:
- tokens: bfloat16 [4, 256, 128, 1152], P('img', 'row', 'col'), may hold values from -30 to 30
- qkv_weight: bfloat16 [1152, 1728], replicated, may hold values from -1 to 1
- out_weight: bfloat16 [1152, 576], replicated, may hold values from -0.25 to 0.25
- upstream: bfloat16 [4, 256, 128, 1152], P('img', 'row', 'col'), may hold values from -6 to 6
Outputs:
- sublayer_out: bfloat16 [4, 256, 128, 1152], P('img', 'row', 'col')
- tokens_grad: bfloat16 [4, 256, 128, 1152], P('img', 'row', 'col')
- qkv_grad: float32 [1152, 1728], P(('row', 'col'))
- out_grad: float32 [1152, 576], P(('row', 'col'))
All inputs are finite; a program needn't handle non-finite values.
Results may differ from a plain program's by a relative error of at most 0.015.
Values may be sent and summed in bfloat16 or wider, within the bound.
A program may use at most 128 MiB of HBM per device.

v0:
```python
import jax
import jax.numpy as jnp
from jax import lax
from jax.sharding import PartitionSpec as P

H = 8
DH = 72
REACH = 8
WINDOW = 17


masked_score = -1e30
query_side = 8


def with_halo(block, sides, width):
    for axis, dim in sides:
        count = lax.axis_size(axis)
        forward = [(i, i + 1) for i in range(count - 1)]
        backward = [(target, source) for source, target in forward]
        low = lax.ppermute(
            lax.slice_in_dim(block, block.shape[dim] - width, None, axis=dim), axis, forward
        )
        high = lax.ppermute(lax.slice_in_dim(block, 0, width, axis=dim), axis, backward)
        block = jnp.concatenate([low, block, high], axis=dim)
    return block


def passed_along(shard, axis, by):
    devices = lax.axis_size(axis)
    pairs = [(i, i + by) for i in range(devices) if 0 <= i + by < devices]
    return lax.ppermute(shard, axis, pairs)


def window_starts(first_row, count, extent):
    places = first_row + jnp.arange(count, dtype=jnp.int32)
    return jnp.clip(places - REACH, 0, extent - WINDOW)


def strip_setup(strip_id, tile_rows, tile_cols):
    band_side = query_side + 2 * REACH
    ext_cols = tile_cols + 2 * REACH
    row_first = lax.axis_index("row") * tile_rows
    col_first = lax.axis_index("col") * tile_cols
    frame_rows = tile_rows * lax.axis_size("row")
    frame_cols = tile_cols * lax.axis_size("col")
    glob_row = row_first + strip_id * query_side
    band_row = jnp.clip(glob_row - REACH, 0, frame_rows - WINDOW)
    row_starts = window_starts(glob_row, query_side, frame_rows)
    col_starts = window_starts(col_first, tile_cols, frame_cols)
    key_rows = band_row + jnp.arange(band_side, dtype=jnp.int32)
    key_cols = col_first - REACH + jnp.arange(ext_cols, dtype=jnp.int32)
    row_ok = (key_rows[None, :] >= row_starts[:, None]) & (
        key_rows[None, :] <= row_starts[:, None] + 2 * REACH
    )
    col_ok = (key_cols[None, :] >= col_starts[:, None]) & (
        key_cols[None, :] <= col_starts[:, None] + 2 * REACH
    )
    joined = row_ok[:, None, :, None] & col_ok[None, :, None, :]
    in_window = joined.reshape(query_side * tile_cols, band_side * ext_cols)
    return (band_row - row_first + REACH, in_window)


def cut_band(extended, band_top):
    band_side = query_side + 2 * REACH
    band = lax.dynamic_slice_in_dim(extended, band_top, band_side, 0)
    band = band.reshape(band_side * extended.shape[1], 2, H, DH)
    return (band[:, 0], band[:, 1])


def strip_probs(query_blk, key_band, in_window):
    scores = jnp.einsum(
        "qhd,khd->hqk", query_blk, key_band, preferred_element_type=jnp.float32
    ) * DH ** (-0.5)
    scores = jnp.where(in_window[None], scores, masked_score)
    row_max = jnp.max(scores, axis=2, keepdims=True)
    shifted = jnp.exp(scores - row_max)
    return shifted / jnp.sum(shifted, axis=2, keepdims=True)


def local(tokens, qkv_weight, out_weight, upstream):
    tile_rows = tokens.shape[1]
    tile_cols = tokens.shape[2]
    width = tokens.shape[3]
    token_count = tile_rows * tile_cols
    inner = H * DH
    ext_rows = tile_rows + 2 * REACH
    ext_cols = tile_cols + 2 * REACH
    band_side = query_side + 2 * REACH
    strips = tile_rows // query_side
    strip_tokens = query_side * tile_cols
    strip_ids = jnp.arange(strips, dtype=jnp.int32)
    token_rows = tokens.reshape(token_count, width)
    grad_rows = upstream.reshape(token_count, width)
    projected = jnp.dot(token_rows, qkv_weight, preferred_element_type=jnp.float32).astype(
        jnp.bfloat16
    )
    query_strips = projected[:, :inner].reshape(strips, strip_tokens, H, DH)
    keyvals = projected[:, inner:].reshape(1, tile_rows, tile_cols, 2 * inner)
    extended = with_halo(keyvals, (("row", 1), ("col", 2)), REACH)
    extended = extended.reshape(ext_rows, ext_cols, 2 * inner)

    def forward_strip(operands):
        strip_id, query_blk = operands
        band_top, in_window = strip_setup(strip_id, tile_rows, tile_cols)
        key_band, value_band = cut_band(extended, band_top)
        attn_prob = strip_probs(query_blk, key_band, in_window)
        attended_blk = jnp.einsum(
            "hqk,khd->qhd",
            attn_prob.astype(jnp.bfloat16),
            value_band,
            preferred_element_type=jnp.float32,
        )
        return (attended_blk.astype(jnp.bfloat16), attn_prob)

    attended_strips, kept_probs = lax.map(forward_strip, (strip_ids, query_strips))
    attended = attended_strips.reshape(token_count, inner)
    sublayer_out = lax.dot_general(
        attended, out_weight, (((1,), (1,)), ((), ())), preferred_element_type=jnp.float32
    ).astype(jnp.bfloat16)
    grad_att = jnp.dot(grad_rows, out_weight, preferred_element_type=jnp.float32).astype(
        jnp.bfloat16
    )
    grad_strips = grad_att.reshape(strips, strip_tokens, H, DH)

    def backward_strip(accum, strip_id, query_blk, grad_blk, attn_prob):
        band_top, in_window = strip_setup(strip_id, tile_rows, tile_cols)
        key_band, value_band = cut_band(extended, band_top)
        prob_low = attn_prob.astype(jnp.bfloat16)
        dprob = jnp.einsum("qhd,khd->hqk", grad_blk, value_band, preferred_element_type=jnp.float32)
        row_dot = jnp.sum(attn_prob * dprob, axis=2, keepdims=True)
        dscore = (attn_prob * (dprob - row_dot) * DH ** (-0.5)).astype(jnp.bfloat16)
        dquery = jnp.einsum("hqk,khd->qhd", dscore, key_band, preferred_element_type=jnp.float32)
        dkey = jnp.einsum("hqk,qhd->khd", dscore, query_blk, preferred_element_type=jnp.float32)
        dvalue = jnp.einsum("hqk,qhd->khd", prob_low, grad_blk, preferred_element_type=jnp.float32)
        band_grad = jnp.concatenate(
            [dkey.reshape(band_side, ext_cols, inner), dvalue.reshape(band_side, ext_cols, inner)],
            axis=2,
        )
        current = lax.dynamic_slice_in_dim(accum, band_top, band_side, 0)
        accum = lax.dynamic_update_slice_in_dim(accum, current + band_grad, band_top, 0)
        return (accum, dquery)

    empty_grads = jnp.zeros((ext_rows, ext_cols, 2 * inner), jnp.float32)

    def backward_kept(accum, operands):
        strip_id, query_blk, grad_blk, attn_prob = operands
        return backward_strip(accum, strip_id, query_blk, grad_blk, attn_prob)

    returned, dquery_strips = lax.scan(
        backward_kept, empty_grads, (strip_ids, query_strips, grad_strips, kept_probs)
    )
    dquery_rows = dquery_strips.reshape(token_count, inner)
    top_band = returned[:REACH]
    bottom_band = returned[ext_rows - REACH :]
    from_below = passed_along(top_band.astype(jnp.bfloat16), "row", -1).astype(top_band.dtype)
    from_above = passed_along(bottom_band.astype(jnp.bfloat16), "row", 1).astype(bottom_band.dtype)
    inner_rows = returned[REACH : ext_rows - REACH]
    inner_rows = inner_rows.at[:REACH].add(from_above).at[tile_rows - REACH :].add(from_below)
    left_band = inner_rows[:, :REACH]
    right_band = inner_rows[:, ext_cols - REACH :]
    from_right = passed_along(left_band.astype(jnp.bfloat16), "col", -1).astype(left_band.dtype)
    from_left = passed_along(right_band.astype(jnp.bfloat16), "col", 1).astype(right_band.dtype)
    middle = inner_rows[:, REACH : ext_cols - REACH]
    middle = middle.at[:, :REACH].add(from_left).at[:, tile_cols - REACH :].add(from_right)
    dqkv = jnp.concatenate([dquery_rows, middle.reshape(token_count, 2 * inner)], axis=1).astype(
        jnp.bfloat16
    )
    tokens_grad = lax.dot_general(
        dqkv, qkv_weight, (((1,), (1,)), ((), ())), preferred_element_type=jnp.float32
    ).astype(jnp.bfloat16)
    first_term = lax.dot_general(
        token_rows, dqkv, (((0,), (0,)), ((), ())), preferred_element_type=jnp.float32
    )
    second_term = lax.dot_general(
        grad_rows, attended, (((0,), (0,)), ((), ())), preferred_element_type=jnp.float32
    )
    shares = lax.psum_scatter(
        jnp.concatenate([first_term, second_term], axis=1),
        ("row", "col"),
        scatter_dimension=0,
        tiled=True,
    )
    shares = lax.psum(shares.astype(jnp.bfloat16), "img").astype(jnp.float32)
    return (
        sublayer_out.reshape(tokens.shape),
        tokens_grad.reshape(tokens.shape),
        shares[:, : 3 * inner],
        shares[:, 3 * inner :],
    )


def solution(mesh):
    return jax.shard_map(
        local,
        mesh=mesh,
        in_specs=(P("img", "row", "col", None), P(), P(), P("img", "row", "col", None)),
        out_specs=(
            P("img", "row", "col", None),
            P("img", "row", "col", None),
            P(("row", "col"), None),
            P(("row", "col"), None),
        ),
        check_vma=False,
    )
```

profile of v0, /device:TPU:1, one launch (start us, length us, event | category | flops | bytes accessed | tf_op | source)
XLA Modules:
  0.0 848.8 jit_solution(2331634278644326645)
XLA Ops:
  7.2 5.1 convolution_convert_fusion
  16.3 4.0 collective-permute-start
  21.7 4.3 collective-permute-done
  26.0 3.8 collective-permute-done.1
  32.2 5.3 collective-permute-start.2
  48.1 5.0 collective-permute-done.2
  53.1 4.0 maximum_bitcast_fusion
  57.1 127.8 %while.33 = (s32[]{:T(128)}, bf16[4,128,8,72]{1,3,2,0:T(8,128)(2,1)}, f32[4,8,128,768]{3,2,1,0:T(8,128)}, s32[4]{0:T(128)S(1)}, bf16[48,32,1152]{2,1,0:T(8,128)(...) while((s32[]{:T(128)}, ...), condition=%wide.region_3.4_spmd, body=%wide.region_0.3_spmd.sunk | while | flops 233745376 | bytes 48087144 | solution.py:116
  60.0 6.4 reshape.376
  76.8 4.3 fusion.107
  85.5 3.6 fusion.108
  91.9 6.4 reshape.376
  108.8 4.3 fusion.107
  117.4 3.6 fusion.108
  123.9 6.4 reshape.376
  136.2 3.5 fusion.106
  140.7 4.3 fusion.107
  149.4 3.6 fusion.108
  155.8 6.4 reshape.376
  168.2 3.5 fusion.106
  172.7 4.3 fusion.107
  181.3 3.6 fusion.108
  184.9 3.7 broadcast_in_dim.71
  188.6 224.8 %while.34 = (s32[]{:T(128)}, f32[48,32,1152]{2,1,0:T(8,128)}, bf16[4,128,8,72]{1,3,2,0:T(8,128)(2,1)}, s32[4]{0:T(128)S(1)}, bf16[4,128,8,72]{1,3,2,0:T(8,128)(2...) while((s32[]{:T(128)}, f32[48,32,1152]{2,1,0:T(8,128)}, ...), condition=%wide.region_6.7_spmd, body=%wide.region_4.6_spmd.sunk | while | flops 571934464 | bytes 75894736 | solution.py:150
  191.4 6.4 reshape.378
  197.8 3.8 fusion.117
  204.6 4.3 fusion.118
  208.9 3.8 fusion.119
  218.5 4.1 reshape.379
  222.6 3.6 fusion.116
  229.6 4.1 reshape.377
  233.6 5.7 fusion.120
  247.6 6.4 reshape.378
  254.0 3.8 fusion.117
  260.7 4.3 fusion.118
  265.0 3.8 fusion.119
  274.7 4.1 reshape.379
  278.8 3.6 fusion.116
  285.7 4.1 reshape.377
  289.8 5.7 fusion.120
  303.8 6.4 reshape.378
  310.2 3.8 fusion.117
  316.9 4.3 fusion.118
  321.2 3.8 fusion.119
  330.9 4.1 reshape.379
  334.9 3.6 fusion.116
  341.9 4.1 reshape.377
  346.0 5.7 fusion.120
  360.0 6.4 reshape.378
  366.4 3.8 fusion.117
  373.1 4.3 fusion.118
  377.4 3.8 fusion.119
  387.1 4.1 reshape.379
  391.2 3.6 fusion.116
  398.1 4.1 reshape.377
  402.2 5.7 fusion.120
  428.5 6.9 collective-permute-done.5
  438.9 5.6 collective-permute-start.6
  454.7 6.5 collective-permute-done.6
  464.2 6.0 convolution_bitcast_fusion.2
  470.2 8.8 %pad_maximum_fusion = f32[1152,2304]{0,1:T(8,128)} fusion(f32[1152,576]{0,1:T(8,128)} %convolution_bitcast_fusion.3, f32[1152,1728]{0,1:T(8,128)} %convolution_bitcast_fusion.2), kind=kLoop, calls=%fused_computation.62 | loop fusion | flops 2654208 | bytes 21233664 | tf_op jit(solution)/shard_map/concatenate | solution.py:179
  479.0 291.7 %all-reduce.5 = bf16[1152,2304]{0,1:T(8,128)(2,1)} all-reduce(f32[1152,2304]{0,1:T(8,128)} %pad_maximum_fusion), channel_id=2, replica_groups=mesh['img'=4,'row'=8,'col'=8] {'row','col'}, use_global_device_ids=true, to_apply=%region_7.8.clone | all-reduce | flops 2654208 | bytes 15925248
  773.0 5.7 convolution_convert_fusion.1
  778.8 59.4 %all-reduce.4.cloned.1.call-done = bf16[18,2304]{0,1:T(8,128)(2,1)} async-done(((bf16[18,2304]{0,1:T(8,128)(2,1)}), bf16[18,2304]{0,1:T(8,128)(2,1)}) %all-reduce.4.cloned.1.call-update) | async-done | bytes 82960 | tf_op jit(solution)/shard_map/psum | solution.py:184
  (197 shorter events, 195.6 us)
Async XLA Ops:
  7.2 35.4 %copy-start = (bf16[1152,576]{0,1:T(8,128)(2,1)S(1)}, bf16[1152,576]{0,1:T(8,128)(2,1)}, u32[]{:S(2)}) copy-start(bf16[1152,576]{0,1:T(8,128)(2,1)} %param.18) | copy-start | bytes 3981316
  7.2 831.0 %all-reduce.4.cloned.1.call-start = ((), (), s32[]{:S(2)}) async-start(), calls=%async_computation | async-start | bytes 1179648 | tf_op jit(solution)/shard_map/psum | solution.py:184
  12.3 1.2 copy-start.5
  16.3 9.7 %collective-permute-start = (bf16[1,8,16,1152]{3,2,1,0:T(8,128)(2,1)S(1)}, bf16[1,8,16,1152]{3,2,1,0:T(8,128)(2,1)S(1)}, u32[]{:S(2)}, u32[]{:S(2)}) collective-permute-start(bf16[1,8,16,1152]{3,2,1,0:T(8,128)(2,1)S(1)} %get-tuple-element.358), channel_id=1, source_target_pairs={{0,8},{8,16},{16,24},{24,32},{32,40},{40,48},{48,56},{1,9},{9,17},... | collective-permute-start | bytes 884744 | tf_op jit(solution)/shard_map/ppermute | solution.py:21
  20.4 9.5 %collective-permute-start.1 = (bf16[1,8,16,1152]{3,2,1,0:T(8,128)(2,1)S(1)}, bf16[1,8,16,1152]{3,2,1,0:T(8,128)(2,1)S(1)}, u32[]{:S(2)}, u32[]{:S(2)}) collective-permute-start(bf16[1,8,16,1152]{3,2,1,0:T(8,128)(2,1)S(1)} %get-tuple-element.359), channel_id=1, source_target_pairs={{8,0},{16,8},{24,16},{32,24},{40,32},{48,40},{56,48},{9,1},{17,9},... | collective-permute-start | bytes 884744 | tf_op jit(solution)/shard_map/ppermute | solution.py:24
  29.8 0.7 copy-start.6
  30.8 8.8 %slice-start = ((bf16[512,1728]{0,1:T(8,128)(2,1)}), bf16[512,576]{0,1:T(8,128)(2,1)S(1)}, s32[]{:S(2)}) async-start(bf16[512,1728]{0,1:T(8,128)(2,1)} %copy-done.5), calls=%async_computation.1 | async-start | bytes 1179648 | tf_op jit(solution)/shard_map/slice | solution.py:98
  32.2 20.9 %collective-permute-start.2 = (bf16[1,48,8,1152]{3,2,1,0:T(8,128)(2,1)}, bf16[1,48,8,1152]{3,2,1,0:T(8,128)(2,1)}, u32[]{:S(2)}, u32[]{:S(2)}) collective-permute-start(bf16[1,48,8,1152]{3,2,1,0:T(8,128)(2,1)} %get-tuple-element.356), channel_id=1, source_target_pairs={{0,1},{1,2},{2,3},{3,4},{4,5},{5,6},{6,7},{8,9},{9,10},{10,11},{11... | collective-permute-start | bytes 2654216 | tf_op jit(solution)/shard_map/ppermute | solution.py:21
  37.5 15.6 %collective-permute-start.3 = (bf16[1,48,8,1152]{3,2,1,0:T(8,128)(2,1)}, bf16[1,48,8,1152]{3,2,1,0:T(8,128)(2,1)}, u32[]{:S(2)}, u32[]{:S(2)}) collective-permute-start(bf16[1,48,8,1152]{3,2,1,0:T(8,128)(2,1)} %get-tuple-element.357), channel_id=1, source_target_pairs={{1,0},{2,1},{3,2},{4,3},{5,4},{6,5},{7,6},{9,8},{10,9},{11,10},{12... | collective-permute-start | bytes 2654216 | tf_op jit(solution)/shard_map/ppermute | solution.py:24
  81.1 2.6 copy-start.2
  113.1 2.6 copy-start.2
  145.0 2.6 copy-start.2
  177.0 2.6 copy-start.2
  197.8 6.7 copy-start.4
  203.7 0.9 copy-start.1
  233.6 8.4 copy-start.8
  243.9 0.9 copy-start.9
  254.0 6.7 copy-start.4
  259.8 0.9 copy-start.1
  289.8 8.4 copy-start.8
  300.1 0.9 copy-start.9
  310.2 6.7 copy-start.4
  316.0 0.9 copy-start.1
  346.0 8.5 copy-start.8
  356.3 0.9 copy-start.9
  366.4 6.7 copy-start.4
  372.2 0.9 copy-start.1
  402.2 8.4 copy-start.8
  412.5 0.9 copy-start.9
  413.3 8.0 copy-start.13
  416.9 10.0 %collective-permute-start.4 = (bf16[8,32,1152]{2,1,0:T(8,128)(2,1)S(1)}, bf16[8,32,1152]{2,1,0:T(8,128)(2,1)}, u32[]{:S(2)}, u32[]{:S(2)}) collective-permute-start(bf16[8,32,1152]{2,1,0:T(8,128)(2,1)S(1)} %get-tuple-element.353), channel_id=1, source_target_pairs={{0,8},{8,16},{16,24},{24,32},{32,40},{40,48},{48,56},{1,9},{9,17},... | collective-permute-start | bytes 1769480 | tf_op jit(solution)/shard_map/ppermute | solution.py:32
  420.0 15.4 %collective-permute-start.5 = (bf16[8,32,1152]{2,1,0:T(8,128)(2,1)S(1)}, bf16[8,32,1152]{2,1,0:T(8,128)(2,1)S(1)}, u32[]{:S(2)}, u32[]{:S(2)}) collective-permute-start(bf16[8,32,1152]{2,1,0:T(8,128)(2,1)S(1)} %get-tuple-element.352), channel_id=1, source_target_pairs={{8,0},{16,8},{24,16},{32,24},{40,32},{48,40},{56,48},{9,1},{17,9},... | collective-permute-start | bytes 1769480 | tf_op jit(solution)/shard_map/ppermute | solution.py:32
  422.6 2.7 copy-start.11
  435.7 2.1 copy-start.3
  435.7 8.9 %copy-start.7 = (bf16[1,32,16,1152]{3,2,1,0:T(8,128)(2,1)S(1)}, bf16[1,32,16,1152]{3,2,1,0:T(8,128)(2,1)}, u32[]{:S(2)}) copy-start(bf16[1,32,16,1152]{3,2,1,0:T(8,128)(2,1)} %param.19) | copy-start | bytes 3538948
  438.9 22.2 %collective-permute-start.6 = (bf16[32,8,1152]{2,1,0:T(8,128)(2,1)}, bf16[32,8,1152]{2,1,0:T(8,128)(2,1)}, u32[]{:S(2)}, u32[]{:S(2)}) collective-permute-start(bf16[32,8,1152]{2,1,0:T(8,128)(2,1)} %get-tuple-element.355), channel_id=1, source_target_pairs={{0,1},{1,2},{2,3},{3,4},{4,5},{5,6},{6,7},{8,9},{9,10},{10,11},{11... | collective-permute-start | bytes 1769480 | tf_op jit(solution)/shard_map/ppermute | solution.py:32
  447.0 4.3 copy-start.10
  447.0 15.6 %collective-permute-start.7 = (bf16[32,8,1152]{2,1,0:T(8,128)(2,1)}, bf16[32,8,1152]{2,1,0:T(8,128)(2,1)}, u32[]{:S(2)}, u32[]{:S(2)}) collective-permute-start(bf16[32,8,1152]{2,1,0:T(8,128)(2,1)} %get-tuple-element.354), channel_id=1, source_target_pairs={{1,0},{2,1},{3,2},{4,3},{5,4},{6,5},{7,6},{9,8},{10,9},{11,10},{12... | collective-permute-start | bytes 1769480 | tf_op jit(solution)/shard_map/ppermute | solution.py:32
  462.7 1.5 copy-start.12
Sparse Core Ops, SparseCore 0:
  773.2 64.9 all-reduce.3
where the time goes:
time: 853 us; the launch traced here: 849 us
  blocking collectives  292 us (34%)
  local copies, waits for them, and re-layouts  236 us (28%)
  matrix products  117 us (14%)
  waiting for transfers between devices  87.1 us (10%)
  other arithmetic  71.9 us (8%)
  starting transfers between devices  24.8 us (3%)
  between operations  15 us (2%)
    unnamed x1, blocking collectives  292 us
    psum x1, waiting for transfers between devices, local(): shares = lax.psum(shares.astype(jnp.bfloat16), 'img').astype(jnp.float32)  59.4 us
    reshape x8, local copies, waits for them, and re-layouts, cut_band(): band = band.reshape(band_side * extended.shape[1], 2, H, DH)  51.2 us
    while x56, local copies, waits for them, and re-layouts  45.6 us
    slice x8, local copies, waits for them, and re-layouts, cut_band(): return (band[:, 0], band[:, 1])  28.1 us
    dynamic_update_slice x4, other arithmetic, backward_strip(): lax.dynamic_update_slice_in_dim(accum, current + band_grad, band_top, 0)  22.8 us
    sub x4, matrix products, backward_strip(): dscore = (attn_prob * (dprob - row_dot) * DH ** (-0.5)).astype(jnp.bfloat16)  17.2 us
    sub x4, other arithmetic, strip_probs(): shifted = jnp.exp(scores - row_max)  17.1 us
  transfers between devices with their start and end apart: 9, of which 7 were waited for; matrix products, arithmetic and copies ran while one was open for 3% of the time, Pallas kernels for 0%

commit v1 on v0

v1 whole, which is shorter than its diff:
```python
import functools

import jax
import jax.numpy as jnp
from jax import lax
from jax.experimental import pallas as pl
from jax.experimental.pallas import tpu as pltpu
from jax.sharding import PartitionSpec as P

H = 8
DH = 72
REACH = 8
WINDOW = 17
INNER = H * DH
PAIRS = H // 2
SPAN = 256
WIDE = 640
SHIFT = 64

masked_score = -1e30
bf16 = jnp.bfloat16
f32 = jnp.float32
MESH = pl.DeviceIdType.MESH
VMEM_SPEC = pl.BlockSpec(memory_space=pltpu.VMEM)
ANY_SPEC = pl.BlockSpec(memory_space=pl.ANY)


def mm(a, b):
    return jnp.dot(a, b, preferred_element_type=f32)


def by_column_block(rows):
    count, width = rows.shape
    parts = rows.reshape(count // 16, 2, 8, width)
    return [parts[:, j].reshape(count // 2, width) for j in range(2)]


def project_kernel(tok_ref, up_ref, wqkv_ref, wout_ref, q_ref, kv_ref, ga_ref):
    x = tok_ref[...]
    query = by_column_block(mm(x, wqkv_ref[:, :WIDE]))
    key = by_column_block(mm(x, wqkv_ref[:, 512 : 2 * INNER])[:, SHIFT:])
    value = by_column_block(mm(x, wqkv_ref[:, 2 * INNER :]))
    for j in range(2):
        q_ref[j] = query[j].astype(bf16)
        kv_ref[j] = jnp.concatenate([key[j], value[j]], axis=1).astype(bf16)
    grads = by_column_block(mm(up_ref[...], wout_ref[...]))
    for j in range(2):
        blank = jnp.zeros((grads[j].shape[0], SHIFT), f32)
        ga_ref[j] = jnp.concatenate([blank, grads[j]], axis=1).astype(bf16)


def project(token_rows, grad_rows, qkv_weight, out_weight):
    half = token_rows.shape[0] // 2
    return pl.pallas_call(
        project_kernel,
        out_shape=(
            jax.ShapeDtypeStruct((2, half, WIDE), bf16),
            jax.ShapeDtypeStruct((2, half, 2 * INNER), bf16),
            jax.ShapeDtypeStruct((2, half, WIDE), bf16),
        ),
        in_specs=[VMEM_SPEC] * 4,
        out_specs=(VMEM_SPEC,) * 3,
        compiler_params=pltpu.CompilerParams(vmem_limit_bytes=48 * 2**20),
        name="project",
    )(token_rows, grad_rows, qkv_weight, out_weight)


AROUND = [(dr, dc) for dr in (-1, 0, 1) for dc in (-1, 0, 1) if (dr, dc) != (0, 0)]


def halo_part(dr, dc):
    blocks = {-1: slice(0, 1), 0: slice(1, 3), 1: slice(3, 4)}[dc]
    tokens = {-1: slice(0, 64), 0: slice(64, 320), 1: slice(320, 384)}[dr]
    return blocks, tokens


def owned_part(dr, dc):
    blocks = {-1: slice(1, 2), 0: slice(0, 2), 1: slice(0, 1)}[dc]
    tokens = {-1: slice(192, 256), 0: slice(0, 256), 1: slice(0, 64)}[dr]
    return blocks, tokens


def size_of(part):
    return tuple(s.stop - s.start for s in part)


def place():
    return lax.axis_index("row"), lax.axis_index("col")


def inside(row, col):
    rows, cols = lax.axis_size("row"), lax.axis_size("col")
    return (row >= 0) & (row < rows) & (col >= 0) & (col < cols)


def greet_around(row, col):
    barrier = pltpu.get_barrier_semaphore()
    count = jnp.int32(0)
    for dr, dc in AROUND:
        there = inside(row + dr, col + dc)
        count = count + there.astype(jnp.int32)

        @pl.when(there)
        def _():
            pl.semaphore_signal(
                barrier,
                inc=1,
                device_id={"row": row + dr, "col": col + dc},
                device_id_type=MESH,
            )

    pl.semaphore_wait(barrier, count)


def halo_kernel(kv_ref, ext_ref, zeros, send_sem, recv_sem, local_sem):
    row, col = place()
    greet_around(row, col)

    def sending(n):
        dr, dc = AROUND[n]
        return pltpu.make_async_remote_copy(
            src_ref=kv_ref.at[owned_part(dr, dc)],
            dst_ref=ext_ref.at[halo_part(dr, dc)],
            send_sem=send_sem.at[n],
            recv_sem=recv_sem.at[n],
            device_id={"row": row - dr, "col": col - dc},
            device_id_type=MESH,
        )

    for n, (dr, dc) in enumerate(AROUND):

        @pl.when(inside(row - dr, col - dc))
        def _():
            sending(n).start()

    own = pltpu.make_async_copy(kv_ref, ext_ref.at[1:3, 64:320], local_sem.at[8])
    own.start()
    zeros[...] = jnp.zeros_like(zeros)

    def blanking(n):
        part = halo_part(*AROUND[n])
        blocks, tokens = size_of(part)
        return pltpu.make_async_copy(
            zeros.at[:blocks, :tokens], ext_ref.at[part], local_sem.at[n]
        )

    for n, (dr, dc) in enumerate(AROUND):

        @pl.when(jnp.logical_not(inside(row + dr, col + dc)))
        def _():
            blanking(n).start()

    for n, (dr, dc) in enumerate(AROUND):

        @pl.when(inside(row + dr, col + dc))
        def _():
            sending(n).wait_recv()

        @pl.when(jnp.logical_not(inside(row + dr, col + dc)))
        def _():
            blanking(n).wait()

    for n, (dr, dc) in enumerate(AROUND):

        @pl.when(inside(row - dr, col - dc))
        def _():
            sending(n).wait_send()

    own.wait()


def with_halo(kv):
    return pl.pallas_call(
        halo_kernel,
        out_shape=jax.ShapeDtypeStruct((4, 384, 2 * INNER), bf16),
        in_specs=[ANY_SPEC],
        out_specs=ANY_SPEC,
        scratch_shapes=[
            pltpu.VMEM((2, 256, 2 * INNER), bf16),
            pltpu.SemaphoreType.DMA((8,)),
            pltpu.SemaphoreType.DMA((8,)),
            pltpu.SemaphoreType.DMA((9,)),
        ],
        compiler_params=pltpu.CompilerParams(collective_id=0, has_side_effects=True),
        name="halo",
    )(kv)


def attention_kernel(
    cols_bound, rows_bound, ext_ref, q_ref, ga_ref, att_ref, dq_ref, dkv_ref,
    grads, k_turned, v_turned, bias, att_sum, dq_sum,
):
    row, col = place()
    row_first, col_first = row * 32, col * 16
    last_col = lax.axis_size("col") - 1
    exp_scale = DH ** (-0.5) * 1.4426950408889634

    for p in range(PAIRS):
        for cb in range(4):
            k_turned[p, cb] = ext_ref[cb, :, pl.ds(128 * p, SPAN)].T
            v_turned[p, cb] = ext_ref[cb, :, pl.ds(512 + 128 * p, SPAN)].T
    grads[...] = jnp.zeros_like(grads)
    att_sum[...] = jnp.zeros_like(att_sum)
    dq_sum[...] = jnp.zeros_like(dq_sum)

    at_row = lax.broadcasted_iota(jnp.int32, (SPAN, 128), 0)
    at_lane = lax.broadcasted_iota(jnp.int32, (128, SPAN), 1)

    def head_of(at, first):
        return (at >= first) & (at < first + DH)

    def split_turned(block, first):
        turned = block.T
        none = jnp.zeros_like(turned)
        return jnp.concatenate(
            [jnp.where(head_of(at_row, first + n * DH), turned, none) for n in range(2)], axis=1
        )

    def split_rows(block, first):
        none = jnp.zeros_like(block)
        return jnp.concatenate(
            [jnp.where(head_of(at_lane, first + n * DH), block, none) for n in range(2)], axis=0
        )

    def joined(turned, first):
        kept = jnp.where(
            head_of(at_row, first),
            turned[:, :128],
            jnp.where(head_of(at_row, first + DH), turned[:, 128:], 0.0),
        )
        return kept.T.reshape(16, 8, SPAN)

    def strip(s, _):
        j, t = s // 2, s % 2
        first_cb = jnp.where(col == 0, 1, jnp.where(col == last_col, 0, j))
        at = pl.multiple_of(128 * t, 128)
        band = pl.ds(at, 256)
        key_at = lax.broadcasted_iota(jnp.int32, (256, 128), 0)
        query_at = lax.broadcasted_iota(jnp.int32, (256, 128), 1)
        query_row = row_first + 16 * t + query_at // 8
        query_col = col_first + 8 * j + query_at % 8
        row_start = jnp.clip(query_row - REACH, 0, rows_bound)
        col_start = jnp.clip(query_col - REACH, 0, cols_bound)
        for b in range(3):
            key_row = row_first + 16 * t - REACH + key_at // 8
            key_col = col_first + 8 * (first_cb + b) - REACH + key_at % 8
            seen = (
                (key_row >= row_start)
                & (key_row <= row_start + 2 * REACH)
                & (key_col >= col_start)
                & (key_col <= col_start + 2 * REACH)
            )
            bias[b] = jnp.where(seen, 0.0, masked_score)
        for p in range(PAIRS):
            low, high = 16 * p, SHIFT + 16 * p
            here = pl.ds(128 * p, SPAN)
            there = pl.ds(512 + 128 * p, SPAN)
            query = q_ref[j, pl.ds(at, 128), here]
            upward = ga_ref[j, pl.ds(at, 128), here]
            query_turned = split_turned(query, low)
            upward_turned = split_turned(upward, high)
            scores = []
            for b in range(3):
                hidden = bias[b]
                scores.append(
                    mm(ext_ref[first_cb + b, band, here], query_turned)
                    + jnp.concatenate([hidden, hidden], axis=1)
                )
            top = functools.reduce(
                jnp.maximum, [jnp.max(x, axis=0, keepdims=True) for x in scores]
            )
            shifted = [jnp.exp2((x - top) * exp_scale) for x in scores]
            total = sum(jnp.sum(x, axis=0, keepdims=True) for x in shifted)
            inverse = 1.0 / total
            prob = [x * inverse for x in shifted]
            prob_low = [x.astype(bf16) for x in prob]
            dprob = [mm(ext_ref[first_cb + b, band, there], upward_turned) for b in range(3)]
            row_dot = sum(
                jnp.sum(x * y, axis=0, keepdims=True) for x, y in zip(prob, dprob)
            )
            dscore = [(x * (y - row_dot)).astype(bf16) for x, y in zip(prob, dprob)]
            att = sum(mm(v_turned[p, first_cb + b, :, band], prob_low[b]) for b in range(3))
            dquery = sum(mm(k_turned[p, first_cb + b, :, band], dscore[b]) for b in range(3))
            rows = pl.ds(16 * t, 16)
            att_sum[rows, j, :, here] += joined(att, high)
            dq_sum[rows, j, :, here] += joined(dquery, low)
            query_rows = split_rows(query, low)
            upward_rows = split_rows(upward, high)
            for b in range(3):
                grads[first_cb + b, band, here] += mm(dscore[b], query_rows)
                grads[first_cb + b, band, there] += mm(prob_low[b], upward_rows)
        return 0

    lax.fori_loop(0, 4, strip, 0)
    scale = DH ** (-0.5)
    att_ref[...] = att_sum[...].reshape(att_ref.shape).astype(bf16)
    dq_ref[...] = (dq_sum[...] * scale).reshape(dq_ref.shape).astype(bf16)
    for cb in range(4):
        dkv_ref[cb, :, :INNER] = (grads[cb, :, :INNER] * scale).astype(bf16)
        dkv_ref[cb, :, INNER:] = grads[cb, :, INNER:].astype(bf16)


def attention(ext, query, grad_att):
    rows = 32 * lax.axis_size("row")
    cols = 16 * lax.axis_size("col")
    tokens = 2 * query.shape[1]
    return pl.pallas_call(
        functools.partial(attention_kernel, cols - WINDOW, rows - WINDOW),
        out_shape=(
            jax.ShapeDtypeStruct((tokens, WIDE), bf16),
            jax.ShapeDtypeStruct((tokens, WIDE), bf16),
            jax.ShapeDtypeStruct(ext.shape, bf16),
        ),
        in_specs=[VMEM_SPEC] * 3,
        out_specs=(VMEM_SPEC,) * 3,
        scratch_shapes=[
            pltpu.VMEM(ext.shape, f32),
            pltpu.VMEM((PAIRS, 4, SPAN, 384), bf16),
            pltpu.VMEM((PAIRS, 4, SPAN, 384), bf16),
            pltpu.VMEM((3, 256, 128), f32),
            pltpu.VMEM((32, 2, 8, WIDE), f32),
            pltpu.VMEM((32, 2, 8, WIDE), f32),
        ],
        compiler_params=pltpu.CompilerParams(vmem_limit_bytes=56 * 2**20),
        name="attention",
    )(ext, query, grad_att)


def return_kernel(dkv_ref, out_ref, side, flat, corner, total, send_sem, recv_sem):
    row, col = place()
    greet_around(row, col)
    slots = {}
    for n, (dr, dc) in enumerate(AROUND):
        if dr == 0:
            slots[n] = side.at[pl.ds((dc + 1) // 2, 1)]
        elif dc == 0:
            slots[n] = flat.at[(dr + 1) // 2]
        else:
            slots[n] = corner.at[pl.ds(dr + 1 + (dc + 1) // 2, 1)]

    def sending(n):
        dr, dc = AROUND[n]
        return pltpu.make_async_remote_copy(
            src_ref=dkv_ref.at[halo_part(dr, dc)],
            dst_ref=slots[n],
            send_sem=send_sem.at[n],
            recv_sem=recv_sem.at[n],
            device_id={"row": row + dr, "col": col + dc},
            device_id_type=MESH,
        )

    for n, (dr, dc) in enumerate(AROUND):

        @pl.when(inside(row + dr, col + dc))
        def _():
            sending(n).start()

    total[...] = dkv_ref[1:3, 64:320].astype(f32)
    for n, (dr, dc) in enumerate(AROUND):

        @pl.when(inside(row - dr, col - dc))
        def _():
            sending(n).wait_recv()
            total[owned_part(dr, dc)] += slots[n][...].astype(f32)

    mine = total[...].reshape(2, 32, 8, 2 * INNER)
    for j in range(2):
        out_ref[:, j] = mine[j]

    for n, (dr, dc) in enumerate(AROUND):

        @pl.when(inside(row + dr, col + dc))
        def _():
            sending(n).wait_send()


def returned(dkv):
    out = pl.pallas_call(
        return_kernel,
        out_shape=jax.ShapeDtypeStruct((32, 2, 8, 2 * INNER), f32),
        in_specs=[VMEM_SPEC],
        out_specs=VMEM_SPEC,
        scratch_shapes=[
            pltpu.VMEM((2, 256, 2 * INNER), bf16),
            pltpu.VMEM((2, 2, 64, 2 * INNER), bf16),
            pltpu.VMEM((4, 64, 2 * INNER), bf16),
            pltpu.VMEM((2, 256, 2 * INNER), f32),
            pltpu.SemaphoreType.DMA((8,)),
            pltpu.SemaphoreType.DMA((8,)),
        ],
        compiler_params=pltpu.CompilerParams(
            collective_id=1, has_side_effects=True, vmem_limit_bytes=40 * 2**20
        ),
        name="give_back",
    )(dkv)
    return out.reshape(512, 2 * INNER).astype(bf16)


def weight_kernel(tok_ref, up_ref, dq_ref, dkv_ref, att_ref, g_ref, turned):
    turned[0] = tok_ref[...].T
    turned[1] = up_ref[...].T

    def rows(n, _):
        at = pl.ds(pl.multiple_of(n * 288, 16), 288)
        for g in range(4):
            left = turned[1 if g == 3 else 0, at, :]
            right = (
                dq_ref[...],
                dkv_ref[:, :WIDE],
                dkv_ref[:, 2 * INNER - WIDE :],
                att_ref[...],
            )[g]
            g_ref[pl.ds(2 * n, 2), g] = mm(left, right).reshape(2, 144, WIDE).astype(bf16)
        return 0

    lax.fori_loop(0, 4, rows, 0)


def weight_grads(token_rows, grad_rows, dq, dkv, att):
    tokens, width = token_rows.shape
    return pl.pallas_call(
        weight_kernel,
        out_shape=jax.ShapeDtypeStruct((8, 4, 144, WIDE), bf16),
        in_specs=[VMEM_SPEC] * 5,
        out_specs=VMEM_SPEC,
        scratch_shapes=[pltpu.VMEM((2, width, tokens), bf16)],
        compiler_params=pltpu.CompilerParams(vmem_limit_bytes=48 * 2**20),
        name="weight_grads",
    )(token_rows, grad_rows, dq, dkv, att)


UPPER = 80


def sum_kernel(
    g_ref, out_ref, mine, recv0, rx1, ry1, a1, a2, rx2, ry2, b, rz, w, fin,
    sem0, sem_x1, sem_y1, sem_x2, sem_y2, send_z, recv_z, send_f, recv_f, local_sem,
):
    img = lax.axis_index("img")
    row, col = place()
    z_hi, y = row // 4, row % 4
    z_lo, core = col // 2, col % 2
    z = z_hi * 4 + z_lo
    other = 1 - core

    def device(img=img, z_hi=z_hi, y=y, z_lo=z_lo, core=core):
        return {"img": img, "row": z_hi * 4 + y, "col": z_lo * 2 + core}

    barrier = pltpu.get_barrier_semaphore()
    greeted = [device(core=other)]
    greeted += [device(img=(img + d) % 4) for d in range(1, 4)]
    greeted += [device(img=(img + d) % 4, core=other) for d in range(1, 4)]
    greeted += [device(y=(y + d) % 4) for d in range(1, 4)]
    for d in range(1, 8):
        z_there = (z + d) % 8
        greeted.append(device(z_hi=z_there // 4, z_lo=z_there % 4))
    for target in greeted:
        pl.semaphore_signal(barrier, inc=1, device_id=target, device_id_type=MESH)
    pl.semaphore_wait(barrier, len(greeted))

    def remote(src, dst, send, recv, target):
        return pltpu.make_async_remote_copy(
            src_ref=src, dst_ref=dst, send_sem=send, recv_sem=recv,
            device_id=target, device_id_type=MESH,
        )

    swaps, loads = [], []
    for k in range(4):
        swaps.append(
            remote(g_ref.at[other, k], recv0.at[k], sem0.at[0, k], sem0.at[1, k], device(core=other))
        )
        loads.append(pltpu.make_async_copy(g_ref.at[core, k], mine.at[k], local_sem.at[k]))
        swaps[k].start()
        loads[k].start()
    for k in range(4):
        loads[k].wait()
        swaps[k].wait_recv()

        def add(n, _):
            mine[k, n] = (mine[k, n].astype(f32) + recv0[k, n].astype(f32)).astype(bf16)
            return 0

        lax.fori_loop(0, 4, add, 0)

    first = []
    for d in range(1, 4):
        x_there, y_there = (img + d) % 4, (y + d) % 4
        first.append(
            remote(
                mine.at[:, x_there, :UPPER], rx1.at[d - 1],
                sem_x1.at[0, d - 1], sem_x1.at[1, d - 1], device(img=x_there),
            )
        )
        first.append(
            remote(
                mine.at[y_there, :, UPPER:], ry1.at[d - 1],
                sem_y1.at[0, d - 1], sem_y1.at[1, d - 1], device(y=y_there),
            )
        )
    for copy in first:
        copy.start()
    for copy in first:
        copy.wait_recv()

    def add_first(n, _):
        upper = mine[n, img, :UPPER].astype(f32)
        lower = mine[y, n, UPPER:].astype(f32)
        for d in range(3):
            upper += rx1[d, n].astype(f32)
            lower += ry1[d, n].astype(f32)
        a1[n] = upper.astype(bf16)
        a2[n] = lower.astype(bf16)
        return 0

    lax.fori_loop(0, 4, add_first, 0)

    second = []
    for d in range(1, 4):
        x_there, y_there = (img + d) % 4, (y + d) % 4
        second.append(
            remote(
                a1.at[y_there], ry2.at[d - 1],
                sem_y2.at[0, d - 1], sem_y2.at[1, d - 1], device(y=y_there),
            )
        )
        second.append(
            remote(
                a2.at[x_there], rx2.at[d - 1],
                sem_x2.at[0, d - 1], sem_x2.at[1, d - 1], device(img=x_there),
            )
        )
    for copy in second:
        copy.start()
    for copy in second:
        copy.wait_recv()
    upper = a1[y].astype(f32)
    lower = a2[img].astype(f32)
    for d in range(3):
        upper += ry2[d].astype(f32)
        lower += rx2[d].astype(f32)
    b[:UPPER] = upper.astype(bf16)
    b[UPPER:] = lower.astype(bf16)

    holder = z_hi == core

    def to_chip(n):
        return remote(
            b.at[pl.ds(32 * n, 48)], rz.at[z], send_z.at[n], recv_z.at[z],
            device(z_hi=core, z_lo=n),
        )

    def from_chip(n):
        return remote(
            b.at[pl.ds(0, 48)], rz.at[n], send_z.at[0], recv_z.at[n], device(core=other)
        )

    for n in range(4):

        @pl.when(jnp.logical_not(holder & (z_lo == n)))
        def _():
            to_chip(n).start()

    def to_owner(d, k):
        return remote(
            w.at[pl.ds(16 * k, 32)], fin.at[img], send_f.at[d, k], recv_f.at[img],
            device(img=(img + d) % 4, core=k),
        )

    @pl.when(holder)
    def _():
        for n in range(8):

            @pl.when(z != n)
            def _():
                from_chip(n).wait_recv()

        own = b[pl.ds(pl.multiple_of(32 * z_lo, 32), 48)].astype(f32)
        rz[z] = own.astype(bf16)
        added = rz[0].astype(f32)
        for n in range(1, 8):
            added += rz[n].astype(f32)
        w[...] = added.astype(bf16)
        for d in range(4):
            for k in range(2):

                @pl.when((core != k) | (d != 0))
                def _():
                    to_owner(d, k).start()

        kept = pltpu.make_async_copy(
            w.at[pl.ds(pl.multiple_of(16 * core, 16), 32)], fin.at[img], local_sem.at[4]
        )
        kept.start()
        kept.wait()

    def from_holder(n):
        return remote(
            w.at[pl.ds(0, 32)], fin.at[n], send_f.at[0, 0], recv_f.at[n], device(core=other)
        )

    for n in range(4):

        @pl.when(jnp.logical_not(holder) | (img != n))
        def _():
            from_holder(n).wait_recv()

    out_ref[...] = fin[...]

    for copy in swaps + first + second:
        copy.wait_send()
    for n in range(4):

        @pl.when(jnp.logical_not(holder & (z_lo == n)))
        def _():
            to_chip(n).wait_send()

    @pl.when(holder)
    def _():
        for d in range(4):
            for k in range(2):

                @pl.when((core != k) | (d != 0))
                def _():
                    to_owner(d, k).wait_send()


def sum_over_devices(g):
    rest = UPPER, 144 - UPPER
    dma = pltpu.SemaphoreType.DMA
    return pl.pallas_call(
        sum_kernel,
        out_shape=jax.ShapeDtypeStruct((4, 32, WIDE), bf16),
        in_specs=[ANY_SPEC],
        out_specs=VMEM_SPEC,
        scratch_shapes=[
            pltpu.VMEM((4, 4, 144, WIDE), bf16),
            pltpu.VMEM((4, 4, 144, WIDE), bf16),
            pltpu.VMEM((3, 4, rest[0], WIDE), bf16),
            pltpu.VMEM((3, 4, rest[1], WIDE), bf16),
            pltpu.VMEM((4, rest[0], WIDE), bf16),
            pltpu.VMEM((4, rest[1], WIDE), bf16),
            pltpu.VMEM((3, rest[1], WIDE), bf16),
            pltpu.VMEM((3, rest[0], WIDE), bf16),
            pltpu.VMEM((144, WIDE), bf16),
            pltpu.VMEM((8, 48, WIDE), bf16),
            pltpu.VMEM((48, WIDE), bf16),
            pltpu.VMEM((4, 32, WIDE), bf16),
            dma((2, 4)),
            dma((2, 3)),
            dma((2, 3)),
            dma((2, 3)),
            dma((2, 3)),
            dma((4,)),
            dma((8,)),
            dma((4, 2)),
            dma((4,)),
            dma((5,)),
        ],
        compiler_params=pltpu.CompilerParams(
            collective_id=2, has_side_effects=True, vmem_limit_bytes=40 * 2**20
        ),
        name="sum_over_devices",
    )(g.reshape(2, 4, 4, 144, WIDE))


def local(tokens, qkv_weight, out_weight, upstream):
    count = tokens.shape[1] * tokens.shape[2]
    width = tokens.shape[3]
    token_rows = tokens.reshape(count, width)
    grad_rows = upstream.reshape(count, width)
    query, keyvals, grad_att = project(token_rows, grad_rows, qkv_weight, out_weight)
    extended = with_halo(keyvals)
    att, dq, dkv = attention(extended, query, grad_att)
    nt = (((1,), (1,)), ((), ()))
    sublayer_out = lax.dot_general(
        att[:, SHIFT:], out_weight, nt, preferred_element_type=f32
    ).astype(bf16)
    dkv = returned(dkv)
    dqkv = jnp.concatenate([dq[:, :INNER], dkv], axis=1)
    tokens_grad = lax.dot_general(dqkv, qkv_weight, nt, preferred_element_type=f32).astype(bf16)
    shares = sum_over_devices(weight_grads(token_rows, grad_rows, dq, dkv, att))
    shares = lax.dynamic_slice_in_dim(shares, 2 * lax.axis_index("col"), 18, 1).astype(f32)
    qkv_grad = jnp.concatenate(
        [shares[0, :, :INNER], shares[1, :, :INNER], shares[2, :, SHIFT:]], axis=1
    )
    return (
        sublayer_out.reshape(tokens.shape),
        tokens_grad.reshape(tokens.shape),
        qkv_grad,
        shares[3, :, SHIFT:],
    )


def solution(mesh):
    return jax.shard_map(
        local,
        mesh=mesh,
        in_specs=(P("img", "row", "col", None), P(), P(), P("img", "row", "col", None)),
        out_specs=(
            P("img", "row", "col", None),
            P("img", "row", "col", None),
            P(("row", "col"), None),
            P(("row", "col"), None),
        ),
        check_vma=False,
    )
```

time: 853 us -> 199 us (0.23)
  blocking collectives: 292 us -> 0 us
  local copies, waits for them, and re-layouts: 236 us -> 19.2 us
  Pallas kernels: 0 us -> 170 us
  matrix products: 117 us -> 8.09 us
  waiting for transfers between devices: 87.1 us -> 0 us
  other arithmetic: 71.9 us -> 0.16 us
  starting transfers between devices: 24.8 us -> 0 us
  between operations: 15 us -> 0.72 us
    unnamed x1 -> x0, blocking collectives: 292 us -> none
    pallas_call x0 -> x6, Pallas kernels: none -> 170 us  [the longest x1 75.9 us: sum_over_devices(): pl.pallas_call(sum_kernel, out_shape=jax.ShapeDtypeStruct((4, 32, WIDE),...]
    dot_general x30 -> x2, matrix products: 99.6 us -> 8.09 us  [the longest x1 5.86 us: local(): lax.dot_general(dqkv, qkv_weight, nt, preferred_element_type=f32)]
    reshape x20 -> x0, local copies, waits for them, and re-layouts: 87.7 us -> none  [the longest x8 51.2 us: cut_band(): band = band.reshape(band_side * extended.shape[1], 2, H, DH)]
    psum x1 -> x0, waiting for transfers between devices: 59.4 us -> none  [local(): shares = lax.psum(shares.astype(jnp.bfloat16), 'img').astype(jnp.float32)]
    while x59 -> x0, local copies, waits for them, and re-layouts: 49 us -> none
    slice x20 -> x0, local copies, waits for them, and re-layouts: 40 us -> none  [the longest x8 28.1 us: cut_band(): return (band[:, 0], band[:, 1])]
    dynamic_update_slice x8 -> x0, other arithmetic: 31.4 us -> none  [the longest x4 22.8 us: backward_strip(): lax.dynamic_update_slice_in_dim(accum, current + band_grad, band_top, 0)]
  transfers between devices with their start and end apart: 9 -> 0, of which waited for: 7 -> 0; matrix products, arithmetic and copies ran while one was open for 3% -> 0% of each run, Pallas kernels for 0% -> 0%
where the time goes in v1:
time: 199 us
  Pallas kernels  170 us (85%)
  local copies, waits for them, and re-layouts  19.2 us (10%)
  matrix products  8.09 us (4%)
    pallas_call x1, Pallas kernels, sum_over_devices(): pl.pallas_call(sum_kernel, out_shape=jax.ShapeDtypeStruct((4, 32, WIDE),...  75.9 us
    pallas_call x1, Pallas kernels, with_halo(): pl.pallas_call(halo_kernel, out_shape=jax.ShapeDtypeStruct((4, 384, 2 * I...  41.1 us
    pallas_call x1, Pallas kernels, attention(): pl.pallas_call(functools.partial(attention_kernel, cols - WINDOW, rows -...  24 us
    unnamed x26, local copies, waits for them, and re-layouts  17.8 us
    pallas_call x1, Pallas kernels, returned(): pl.pallas_call(return_kernel, out_shape=jax.ShapeDtypeStruct((32, 2, 8, 2...  15.1 us
    pallas_call x1, Pallas kernels, weight_grads(): pl.pallas_call(weight_kernel, out_shape=jax.ShapeDtypeStruct((8, 4, 144,...  7.53 us
    pallas_call x1, Pallas kernels, project(): pl.pallas_call(project_kernel, out_shape=(jax.ShapeDtypeStruct((2, half,...  6.8 us
    dot_general x1, matrix products, local(): lax.dot_general(dqkv, qkv_weight, nt, preferred_element_type=f32)  5.86 us

profile of v1, /device:TPU:1, one launch (start us, length us, event | category | flops | bytes accessed | tf_op | source)
XLA Modules:
  0.0 198.6 jit_solution(12707849848544760804)
XLA Ops:
  0.6 6.4 %copy.8.wqkv_ref = bf16[1152,1728]{1,0:T(8,128)(2,1)} copy(bf16[1152,1728]{0,1:T(8,128)(2,1)} %param.5) | data formatting | bytes 7962624 | tf_op args[1]
  7.1 0.0 copy-start.1
  7.1 0.0 copy-start.2
  7.1 2.8 %copy.9.wout_ref = bf16[1152,576]{1,0:T(8,128)(2,1)} copy(bf16[1152,576]{0,1:T(8,128)(2,1)} %param.6) | data formatting | bytes 2654208 | tf_op args[2]
  9.8 0.0 copy-done.1
  9.8 0.0 copy-done.2
  9.8 6.8 %project.1 = (bf16[2,256,640]{2,1,0:T(8,128)(2,1)S(1)}, bf16[2,256,1152]{2,1,0:T(8,128)(2,1)S(1)}, bf16[2,256,640]{2,1,0:T(8,128)(2,1)S(1)}) custom-call(bf16[512,1152]{1,0:T(8,128)(2,1)S(1)} %bitcast.20, bf16[512,1152]{1,0:T(8,128)(2,1)S(1)} %bitcast.22, bf16[1152,1728]{1,0:T(8,128)(2,1)} %copy.8.wqkv_ref, bf16[1152,576]{1,0:T(8,128)(2,1)} %copy.9.wout_ref), custom_call_target="tpu_custom_call" | custom-call | tf_op jit(solution)/shard_map/project/pallas_call | solution.py:54
  16.6 0.0 copy-start.4
  16.7 1.0 copy-done.4
  17.7 0.0 copy-start.5
  17.7 0.8 copy-done.5
  18.5 0.0 copy-start.6
  18.5 0.9 copy-done.6
  19.4 41.1 %halo.1.ext_ref = bf16[4,384,1152]{2,1,0:T(8,128)(2,1)} custom-call(bf16[2,256,1152]{2,1,0:T(8,128)(2,1)} %copy-done.4), custom_call_target="tpu_custom_call" | custom-call | tf_op jit(solution)/shard_map/halo/pallas_call | solution.py:173
  60.5 24.0 %attention.1 = (bf16[512,640]{1,0:T(8,128)(2,1)}, bf16[512,640]{1,0:T(8,128)(2,1)}, bf16[4,384,1152]{2,1,0:T(8,128)(2,1)}) custom-call(bf16[4,384,1152]{2,1,0:T(8,128)(2,1)} %halo.1.ext_ref, bf16[2,256,640]{2,1,0:T(8,128)(2,1)} %copy-done.5, bf16[2,256,640]{2,1,0:T(8,128)(2,1)} %copy-done.6), custom_call_target="tpu_custom_call" | custom-call | tf_op jit(solution)/shard_map/attention/pallas_call | solution.py:307
  84.5 0.0 copy-start.3
  84.5 2.0 %copy-done.3 = bf16[4,384,1152]{2,1,0:T(8,128)(2,1)S(1)} copy-done((bf16[4,384,1152]{2,1,0:T(8,128)(2,1)S(1)}, bf16[4,384,1152]{2,1,0:T(8,128)(2,1)}, u32[]{:S(2)}) %copy-start.3) | copy-done | bytes 3538968
  86.5 15.1 %give_back.1 = f32[32,2,8,1152]{3,2,1,0:T(8,128)S(1)} custom-call(bf16[4,384,1152]{2,1,0:T(8,128)(2,1)S(1)} %copy-done.3), custom_call_target="tpu_custom_call" | custom-call | tf_op jit(solution)/shard_map/give_back/pallas_call | solution.py:378
  101.6 0.0 copy-start.7
  101.6 0.0 copy-start.9
  101.6 0.1 convert_element_type.15
  101.7 0.9 copy-done.7
  102.7 0.2 copy-done.9
  102.9 7.5 %weight_grads.1 = bf16[8,4,144,640]{3,2,1,0:T(8,128)(2,1)} custom-call(bf16[512,1152]{1,0:T(8,128)(2,1)S(1)} %bitcast.21, bf16[512,1152]{1,0:T(8,128)(2,1)S(1)} %bitcast.23, bf16[512,640]{1,0:T(8,128)(2,1)S(1)} %copy-done.9, bf16[512,1152]{1,0:T(8,128)(2,1)S(1)} %bitcast.18, bf16[512,640]{1,0:T(8,128)(2,1)S(1)} %copy-done.7), custom_call_target="tpu_custom_call" | custom-call | tf_op jit(solution)/shard_map/weight_grads/pallas_call | solution.py:421
  110.4 0.0 copy-start
  110.4 2.7 %copy-done = bf16[8,4,144,640]{3,2,1,0:T(8,128)(2,1)S(1)} copy-done((bf16[8,4,144,640]{3,2,1,0:T(8,128)(2,1)S(1)}, bf16[8,4,144,640]{3,2,1,0:T(8,128)(2,1)}, u32[]{:S(2)}) %copy-start) | copy-done | bytes 5898264
  113.1 0.0 copy-start.10
  113.1 75.9 %sum_over_devices.1 = bf16[4,32,640]{2,1,0:T(8,128)(2,1)S(1)} custom-call(bf16[2,4,4,144,640]{4,3,2,1,0:T(8,128)(2,1)S(1)} %bitcast.17), custom_call_target="tpu_custom_call" | custom-call | tf_op jit(solution)/shard_map/sum_over_devices/pallas_call | solution.py:630
  189.1 0.7 slice_bitcast_fusion
  189.8 0.8 concatenate.7
  190.5 0.0 copy-done.10
  190.5 0.0 copy-start.8
  190.5 0.0 copy-start.11
  190.5 5.9 %convolution_convert_fusion = bf16[512,1152]{1,0:T(8,128)(2,1)} fusion(bf16[1152,1728]{0,1:T(8,128)(2,1)} %param.5, bf16[512,1152]{1,0:T(8,128)(2,1)S(1)} %bitcast.19, bf16[512,576]{1,0:T(8,128)(2,1)S(1)} %bitcast.24), kind=kOutput, calls=%fused_computation | convolution fusion | flops 2042560512 | bytes 6930432 | tf_op jit(solution)/shard_map/dot_general | solution.py:680
  196.4 0.0 copy-done.8
  196.4 0.0 copy-done.11
  196.4 2.2 %convolution_convert_fusion.1 = bf16[512,1152]{1,0:T(8,128)(2,1)} fusion(bf16[1152,576]{0,1:T(8,128)(2,1)S(1)} %copy-done.11, bf16[512,640]{1,0:T(8,128)(2,1)S(1)} %copy-done.8), kind=kOutput, calls=%fused_computation.1 | convolution fusion | flops 680067072 | bytes 3162112 | tf_op jit(solution)/shard_map/dot_general | solution.py:675
  (1 shorter events, 0.0 us)
Async XLA Ops:
  7.1 2.8 %copy-start.1 = (bf16[1,32,16,1152]{3,2,1,0:T(8,128)(2,1)S(1)}, bf16[1,32,16,1152]{3,2,1,0:T(8,128)(2,1)}, u32[]{:S(2)}) copy-start(bf16[1,32,16,1152]{3,2,1,0:T(8,128)(2,1)} %param.4) | copy-start | bytes 3538948
  7.1 2.8 %copy-start.2 = (bf16[1,32,16,1152]{3,2,1,0:T(8,128)(2,1)S(1)}, bf16[1,32,16,1152]{3,2,1,0:T(8,128)(2,1)}, u32[]{:S(2)}) copy-start(bf16[1,32,16,1152]{3,2,1,0:T(8,128)(2,1)} %param.7) | copy-start | bytes 3538948
  16.6 1.0 copy-start.4
  17.7 0.8 copy-start.5
  18.5 0.9 copy-start.6
  84.5 2.0 %copy-start.3 = (bf16[4,384,1152]{2,1,0:T(8,128)(2,1)S(1)}, bf16[4,384,1152]{2,1,0:T(8,128)(2,1)}, u32[]{:S(2)}) copy-start(bf16[4,384,1152]{2,1,0:T(8,128)(2,1)} %get-tuple-element.15.dkv_ref) | copy-start | bytes 10616836
  101.6 1.1 copy-start.7
  101.6 1.3 copy-start.9
  110.4 2.7 %copy-start = (bf16[8,4,144,640]{3,2,1,0:T(8,128)(2,1)S(1)}, bf16[8,4,144,640]{3,2,1,0:T(8,128)(2,1)}, u32[]{:S(2)}) copy-start(bf16[8,4,144,640]{3,2,1,0:T(8,128)(2,1)} %weight_grads.1) | copy-start | bytes 17694724
  113.1 77.4 %copy-start.10 = (bf16[512,640]{1,0:T(8,128)(2,1)S(1)}, bf16[512,640]{1,0:T(8,128)(2,1)}, u32[]{:S(2)}) copy-start(bf16[512,640]{1,0:T(8,128)(2,1)} %get-tuple-element.14.dq_ref) | copy-start | bytes 1966084
  190.5 5.9 %copy-start.8 = (bf16[512,640]{1,0:T(8,128)(2,1)S(1)}, bf16[512,640]{1,0:T(8,128)(2,1)}, u32[]{:S(2)}) copy-start(bf16[512,640]{1,0:T(8,128)(2,1)} %get-tuple-element.13.att_ref) | copy-start | bytes 1966084
  190.5 5.9 %copy-start.11 = (bf16[1152,576]{0,1:T(8,128)(2,1)S(1)}, bf16[1152,576]{0,1:T(8,128)(2,1)}, u32[]{:S(2)}) copy-start(bf16[1152,576]{0,1:T(8,128)(2,1)} %param.6) | copy-start | bytes 3981316

commit v2 on v1

--- a/solution.py
+++ b/solution.py
@@ -29,6 +29,10 @@
     return jnp.dot(a, b, preferred_element_type=f32)
 
 
+def mm_nt(a, b):
+    return lax.dot_general(a, b, (((1,), (1,)), ((), ())), preferred_element_type=f32)
+
+
 def by_column_block(rows):
     count, width = rows.shape
     parts = rows.reshape(count // 16, 2, 8, width)
@@ -37,13 +41,13 @@
 
 def project_kernel(tok_ref, up_ref, wqkv_ref, wout_ref, q_ref, kv_ref, ga_ref):
     x = tok_ref[...]
-    query = by_column_block(mm(x, wqkv_ref[:, :WIDE]))
-    key = by_column_block(mm(x, wqkv_ref[:, 512 : 2 * INNER])[:, SHIFT:])
-    value = by_column_block(mm(x, wqkv_ref[:, 2 * INNER :]))
+    query = by_column_block(mm_nt(x, wqkv_ref[:WIDE]))
+    key = by_column_block(mm_nt(x, wqkv_ref[INNER : 2 * INNER]))
+    value = by_column_block(mm_nt(x, wqkv_ref[2 * INNER :]))
     for j in range(2):
         q_ref[j] = query[j].astype(bf16)
         kv_ref[j] = jnp.concatenate([key[j], value[j]], axis=1).astype(bf16)
-    grads = by_column_block(mm(up_ref[...], wout_ref[...]))
+    grads = by_column_block(mm_nt(up_ref[...], wout_ref[...]))
     for j in range(2):
         blank = jnp.zeros((grads[j].shape[0], SHIFT), f32)
         ga_ref[j] = jnp.concatenate([blank, grads[j]], axis=1).astype(bf16)
@@ -60,7 +64,7 @@
         ),
         in_specs=[VMEM_SPEC] * 4,
         out_specs=(VMEM_SPEC,) * 3,
-        compiler_params=pltpu.CompilerParams(vmem_limit_bytes=48 * 2**20),
+        compiler_params=pltpu.CompilerParams(vmem_limit_bytes=28 * 2**20),
         name="project",
     )(token_rows, grad_rows, qkv_weight, out_weight)
 
@@ -93,10 +97,13 @@
     return (row >= 0) & (row < rows) & (col >= 0) & (col < cols)
 
 
-def greet_around(row, col):
+BESIDE = [(-1, 0), (1, 0), (0, -1), (0, 1)]
+
+
+def greet_beside(row, col):
     barrier = pltpu.get_barrier_semaphore()
     count = jnp.int32(0)
-    for dr, dc in AROUND:
+    for dr, dc in BESIDE:
         there = inside(row + dr, col + dc)
         count = count + there.astype(jnp.int32)
 
@@ -112,76 +119,88 @@
     pl.semaphore_wait(barrier, count)
 
 
-def halo_kernel(kv_ref, ext_ref, zeros, send_sem, recv_sem, local_sem):
+def halo_kernel(kv_ref, ext_ref, send_sem, recv_sem):
     row, col = place()
-    greet_around(row, col)
+    greet_beside(row, col)
 
     def sending(n):
         dr, dc = AROUND[n]
+        blocks, tokens = halo_part(dr, dc)
+        if dr == 0 or dc == 0:
+            src = kv_ref.at[owned_part(dr, dc)]
+            target = {"row": row - dr, "col": col - dc}
+        else:
+            src = ext_ref.at[{-1: slice(2, 3), 1: slice(1, 2)}[dc], tokens]
+            target = {"row": row, "col": col - dc}
         return pltpu.make_async_remote_copy(
-            src_ref=kv_ref.at[owned_part(dr, dc)],
-            dst_ref=ext_ref.at[halo_part(dr, dc)],
+            src_ref=src,
+            dst_ref=ext_ref.at[blocks, tokens],
             send_sem=send_sem.at[n],
             recv_sem=recv_sem.at[n],
-            device_id={"row": row - dr, "col": col - dc},
+            device_id=target,
             device_id_type=MESH,
         )
 
+    def sends(dr, dc):
+        if dr == 0 or dc == 0:
+            return inside(row - dr, col - dc)
+        return inside(row + dr, col) & inside(row, col - dc)
+
+    index = {way: n for n, way in enumerate(AROUND)}
+    for dr, dc in BESIDE:
+
+        @pl.when(sends(dr, dc))
+        def _():
+            sending(index[dr, dc]).start()
+
+    ext_ref[1:3, 64:320] = kv_ref[...]
+
     for n, (dr, dc) in enumerate(AROUND):
 
-        @pl.when(inside(row - dr, col - dc))
-        def _():
-            sending(n).start()
-
-    own = pltpu.make_async_copy(kv_ref, ext_ref.at[1:3, 64:320], local_sem.at[8])
-    own.start()
-    zeros[...] = jnp.zeros_like(zeros)
-
-    def blanking(n):
-        part = halo_part(*AROUND[n])
-        blocks, tokens = size_of(part)
-        return pltpu.make_async_copy(
-            zeros.at[:blocks, :tokens], ext_ref.at[part], local_sem.at[n]
-        )
+        @pl.when(jnp.logical_not(inside(row + dr, col + dc)))
+        def _():
+            part = halo_part(dr, dc)
+            ext_ref[part] = jnp.zeros(size_of(part) + (2 * INNER,), bf16)
+
+    for dr in (-1, 1):
+
+        @pl.when(inside(row + dr, col))
+        def _():
+            sending(index[dr, 0]).wait_recv()
+
+        for dc in (-1, 1):
+
+            @pl.when(sends(dr, dc))
+            def _():
+                sending(index[dr, dc]).start()
 
     for n, (dr, dc) in enumerate(AROUND):
-
-        @pl.when(jnp.logical_not(inside(row + dr, col + dc)))
-        def _():
-            blanking(n).start()
+        if dc != 0:
+
+            @pl.when(inside(row + dr, col + dc))
+            def _():
+                sending(n).wait_recv()
 
     for n, (dr, dc) in enumerate(AROUND):
 
-        @pl.when(inside(row + dr, col + dc))
-        def _():
-            sending(n).wait_recv()
-
-        @pl.when(jnp.logical_not(inside(row + dr, col + dc)))
-        def _():
-            blanking(n).wait()
-
-    for n, (dr, dc) in enumerate(AROUND):
-
-        @pl.when(inside(row - dr, col - dc))
+        @pl.when(sends(dr, dc))
         def _():
             sending(n).wait_send()
-
-    own.wait()
 
 
 def with_halo(kv):
     return pl.pallas_call(
         halo_kernel,
         out_shape=jax.ShapeDtypeStruct((4, 384, 2 * INNER), bf16),
-        in_specs=[ANY_SPEC],
-        out_specs=ANY_SPEC,
+        in_specs=[VMEM_SPEC],
+        out_specs=VMEM_SPEC,
         scratch_shapes=[
-            pltpu.VMEM((2, 256, 2 * INNER), bf16),
             pltpu.SemaphoreType.DMA((8,)),
             pltpu.SemaphoreType.DMA((8,)),
-            pltpu.SemaphoreType.DMA((9,)),
         ],
-        compiler_params=pltpu.CompilerParams(collective_id=0, has_side_effects=True),
+        compiler_params=pltpu.CompilerParams(
+            collective_id=0, has_side_effects=True, vmem_limit_bytes=12 * 2**20
+        ),
         name="halo",
     )(kv)
 
@@ -321,79 +340,127 @@
             pltpu.VMEM((32, 2, 8, WIDE), f32),
             pltpu.VMEM((32, 2, 8, WIDE), f32),
         ],
-        compiler_params=pltpu.CompilerParams(vmem_limit_bytes=56 * 2**20),
+        compiler_params=pltpu.CompilerParams(vmem_limit_bytes=36 * 2**20),
         name="attention",
     )(ext, query, grad_att)
 
 
-def return_kernel(dkv_ref, out_ref, side, flat, corner, total, send_sem, recv_sem):
+PIECES = [(0, 64), (320, 64), (64, 256)]
+
+
+def return_kernel(dkv_ref, out_ref, side, up_down, flat, total, send_col, recv_col, send_row, recv_row):
     row, col = place()
-    greet_around(row, col)
-    slots = {}
-    for n, (dr, dc) in enumerate(AROUND):
-        if dr == 0:
-            slots[n] = side.at[pl.ds((dc + 1) // 2, 1)]
-        elif dc == 0:
-            slots[n] = flat.at[(dr + 1) // 2]
-        else:
-            slots[n] = corner.at[pl.ds(dr + 1 + (dc + 1) // 2, 1)]
-
-    def sending(n):
-        dr, dc = AROUND[n]
+    greet_beside(row, col)
+
+    def to_side(k, piece):
+        first, size = PIECES[piece]
         return pltpu.make_async_remote_copy(
-            src_ref=dkv_ref.at[halo_part(dr, dc)],
-            dst_ref=slots[n],
-            send_sem=send_sem.at[n],
-            recv_sem=recv_sem.at[n],
-            device_id={"row": row + dr, "col": col + dc},
+            src_ref=dkv_ref.at[3 * k, pl.ds(first, size)],
+            dst_ref=side.at[k, pl.ds(first, size)],
+            send_sem=send_col.at[k, piece],
+            recv_sem=recv_col.at[k, piece],
+            device_id={"row": row, "col": col + 2 * k - 1},
             device_id_type=MESH,
         )
 
-    for n, (dr, dc) in enumerate(AROUND):
-
-        @pl.when(inside(row + dr, col + dc))
-        def _():
-            sending(n).start()
-
-    total[...] = dkv_ref[1:3, 64:320].astype(f32)
-    for n, (dr, dc) in enumerate(AROUND):
-
-        @pl.when(inside(row - dr, col - dc))
-        def _():
-            sending(n).wait_recv()
-            total[owned_part(dr, dc)] += slots[n][...].astype(f32)
-
-    mine = total[...].reshape(2, 32, 8, 2 * INNER)
-    for j in range(2):
-        out_ref[:, j] = mine[j]
-
-    for n, (dr, dc) in enumerate(AROUND):
-
-        @pl.when(inside(row + dr, col + dc))
-        def _():
-            sending(n).wait_send()
+    def to_row(k):
+        return pltpu.make_async_remote_copy(
+            src_ref=up_down.at[k],
+            dst_ref=flat.at[k],
+            send_sem=send_row.at[k],
+            recv_sem=recv_row.at[k],
+            device_id={"row": row + 2 * k - 1, "col": col},
+            device_id_type=MESH,
+        )
+
+    def has_col(k):
+        return inside(row, col + 2 * k - 1)
+
+    def has_row(k):
+        return inside(row + 2 * k - 1, col)
+
+    for piece in range(3):
+        for k in range(2):
+
+            @pl.when(has_col(k))
+            def _():
+                to_side(k, piece).start()
+
+    def gather(piece):
+        first, size = PIECES[piece]
+        at = pl.ds(first, size)
+        total[:, at] = dkv_ref[1:3, at].astype(f32)
+        for k in range(2):
+
+            @pl.when(has_col(1 - k))
+            def _():
+                to_side(k, piece).wait_recv()
+                total[1 - k, at] += side[k, at].astype(f32)
+
+    for k in range(2):
+
+        @pl.when(has_row(k))
+        def _():
+            gather(k)
+            first, size = PIECES[k]
+            up_down[k] = total[:, pl.ds(first, size)].astype(bf16)
+            to_row(k).start()
+
+        @pl.when(jnp.logical_not(has_row(k)))
+        def _():
+            for m in range(2):
+
+                @pl.when(has_col(1 - m))
+                def _():
+                    to_side(m, k).wait_recv()
+
+    gather(2)
+    for k in range(2):
+
+        @pl.when(has_row(1 - k))
+        def _():
+            to_row(k).wait_recv()
+            first = 64 if k == 1 else 256
+            total[:, pl.ds(first, 64)] += flat[k].astype(f32)
+
+    mine = total[:, 64:320].reshape(2, 32, 8, 2 * INNER)
+    out_ref[...] = jnp.stack([mine[0], mine[1]], axis=1).reshape(out_ref.shape).astype(bf16)
+
+    for k in range(2):
+
+        @pl.when(has_row(k))
+        def _():
+            to_row(k).wait_send()
+
+        for piece in range(3):
+
+            @pl.when(has_col(k))
+            def _():
+                to_side(k, piece).wait_send()
 
 
 def returned(dkv):
     out = pl.pallas_call(
         return_kernel,
-        out_shape=jax.ShapeDtypeStruct((32, 2, 8, 2 * INNER), f32),
+        out_shape=jax.ShapeDtypeStruct((512, 2 * INNER), bf16),
         in_specs=[VMEM_SPEC],
         out_specs=VMEM_SPEC,
         scratch_shapes=[
-            pltpu.VMEM((2, 256, 2 * INNER), bf16),
+            pltpu.VMEM((2, 384, 2 * INNER), bf16),
             pltpu.VMEM((2, 2, 64, 2 * INNER), bf16),
-            pltpu.VMEM((4, 64, 2 * INNER), bf16),
-            pltpu.VMEM((2, 256, 2 * INNER), f32),
-            pltpu.SemaphoreType.DMA((8,)),
-            pltpu.SemaphoreType.DMA((8,)),
+            pltpu.VMEM((2, 2, 64, 2 * INNER), bf16),
+            pltpu.VMEM((2, 384, 2 * INNER), f32),
+            pltpu.SemaphoreType.DMA((2, 3)),
+            pltpu.SemaphoreType.DMA((2, 3)),
+            pltpu.SemaphoreType.DMA((2,)),
+            pltpu.SemaphoreType.DMA((2,)),
         ],
         compiler_params=pltpu.CompilerParams(
-            collective_id=1, has_side_effects=True, vmem_limit_bytes=40 * 2**20
+            collective_id=1, has_side_effects=True, vmem_limit_bytes=24 * 2**20
         ),
         name="give_back",
     )(dkv)
-    return out.reshape(512, 2 * INNER).astype(bf16)
+    return out
 
 
 def weight_kernel(tok_ref, up_ref, dq_ref, dkv_ref, att_ref, g_ref, turned):
@@ -424,7 +491,7 @@
         in_specs=[VMEM_SPEC] * 5,
         out_specs=VMEM_SPEC,
         scratch_shapes=[pltpu.VMEM((2, width, tokens), bf16)],
-        compiler_params=pltpu.CompilerParams(vmem_limit_bytes=48 * 2**20),
+        compiler_params=pltpu.CompilerParams(vmem_limit_bytes=24 * 2**20),
         name="weight_grads",
     )(token_rows, grad_rows, dq, dkv, att)
 
@@ -433,7 +500,7 @@
 
 
 def sum_kernel(
-    g_ref, out_ref, mine, recv0, rx1, ry1, a1, a2, rx2, ry2, b, rz, w, fin,
+    g_ref, dq_ref, dkv_ref, att_ref, wqkv_ref, wout_ref, out_ref, tokens_grad_ref, sublayer_ref, mine, recv0, rx1, ry1, a1, a2, rx2, ry2, b, rz, w, fin,
     sem0, sem_x1, sem_y1, sem_x2, sem_y2, send_z, recv_z, send_f, recv_f, local_sem,
 ):
     img = lax.axis_index("img")
@@ -499,6 +566,15 @@
         )
     for copy in first:
         copy.start()
+
+    def products(n, _):
+        at = pl.ds(pl.multiple_of(256 * n, 256), 256)
+        tokens_grad = mm(dq_ref[at, :INNER], wqkv_ref[:INNER]) + mm(dkv_ref[at], wqkv_ref[INNER:])
+        tokens_grad_ref[at] = tokens_grad.astype(bf16)
+        sublayer_ref[at] = mm(att_ref[at, SHIFT:], wout_ref[...]).astype(bf16)
+        return 0
+
+    lax.fori_loop(0, 2, products, 0)
     for copy in first:
         copy.wait_recv()
 
@@ -624,14 +700,18 @@
                     to_owner(d, k).wait_send()
 
 
-def sum_over_devices(g):
+def sum_over_devices(g, dq, dkv, att, qkv_turned, out_turned):
     rest = UPPER, 144 - UPPER
     dma = pltpu.SemaphoreType.DMA
     return pl.pallas_call(
         sum_kernel,
-        out_shape=jax.ShapeDtypeStruct((4, 32, WIDE), bf16),
-        in_specs=[ANY_SPEC],
-        out_specs=VMEM_SPEC,
+        out_shape=(
+            jax.ShapeDtypeStruct((4, 32, WIDE), bf16),
+            jax.ShapeDtypeStruct(dkv.shape, bf16),
+            jax.ShapeDtypeStruct(dkv.shape, bf16),
+        ),
+        in_specs=[ANY_SPEC] + [VMEM_SPEC] * 5,
+        out_specs=(VMEM_SPEC,) * 3,
         scratch_shapes=[
             pltpu.VMEM((4, 4, 144, WIDE), bf16),
             pltpu.VMEM((4, 4, 144, WIDE), bf16),
@@ -660,7 +740,7 @@
             collective_id=2, has_side_effects=True, vmem_limit_bytes=40 * 2**20
         ),
         name="sum_over_devices",
-    )(g.reshape(2, 4, 4, 144, WIDE))
+    )(g.reshape(2, 4, 4, 144, WIDE), dq, dkv, att, qkv_turned, out_turned)
 
 
 def local(tokens, qkv_weight, out_weight, upstream):
@@ -668,17 +748,14 @@
     width = tokens.shape[3]
     token_rows = tokens.reshape(count, width)
     grad_rows = upstream.reshape(count, width)
-    query, keyvals, grad_att = project(token_rows, grad_rows, qkv_weight, out_weight)
+    query, keyvals, grad_att = project(token_rows, grad_rows, qkv_weight.T, out_weight.T)
     extended = with_halo(keyvals)
     att, dq, dkv = attention(extended, query, grad_att)
-    nt = (((1,), (1,)), ((), ()))
-    sublayer_out = lax.dot_general(
-        att[:, SHIFT:], out_weight, nt, preferred_element_type=f32
-    ).astype(bf16)
     dkv = returned(dkv)
-    dqkv = jnp.concatenate([dq[:, :INNER], dkv], axis=1)
-    tokens_grad = lax.dot_general(dqkv, qkv_weight, nt, preferred_element_type=f32).astype(bf16)
-    shares = sum_over_devices(weight_grads(token_rows, grad_rows, dq, dkv, att))
+    grads = weight_grads(token_rows, grad_rows, dq, dkv, att)
+    shares, tokens_grad, sublayer_out = sum_over_devices(
+        grads, dq, dkv, att, qkv_weight.T, out_weight.T
+    )
     shares = lax.dynamic_slice_in_dim(shares, 2 * lax.axis_index("col"), 18, 1).astype(f32)
     qkv_grad = jnp.concatenate(
         [shares[0, :, :INNER], shares[1, :, :INNER], shares[2, :, SHIFT:]], axis=1

time: 199 us -> 153 us (0.77)
  Pallas kernels: 170 us -> 140 us
  matrix products: 8.09 us -> 0 us
  local copies, waits for them, and re-layouts: 19.2 us -> 12 us
    pallas_call x1, Pallas kernels: 41.1 us -> 17 us  [with_halo(): pl.pallas_call(halo_kernel, out_shape=jax.ShapeDtypeStruct((4, 384, 2 * I...]
    dot_general x2 -> x0, matrix products: 8.09 us -> none  [the longest x1 5.86 us: local(): lax.dot_general(dqkv, qkv_weight, nt, preferred_element_type=f32)]
    unnamed x26 -> x20, local copies, waits for them, and re-layouts: 17.8 us -> 10.6 us
    pallas_call x1, Pallas kernels: 24 us -> 19.9 us  [attention(): pl.pallas_call(functools.partial(attention_kernel, cols - WINDOW, rows -...]
    pallas_call x2, Pallas kernels: 91 us -> 94.2 us  [the longest x1 78.9 us: sum_over_devices(): pl.pallas_call(sum_kernel, out_shape=(jax.ShapeDtypeStruct((4, 32, WIDE),...]
    pallas_call x1, Pallas kernels: 6.8 us -> 4.2 us  [project(): pl.pallas_call(project_kernel, out_shape=(jax.ShapeDtypeStruct((2, half,...]
    pallas_call x1, Pallas kernels: 7.53 us -> 5 us  [weight_grads(): pl.pallas_call(weight_kernel, out_shape=jax.ShapeDtypeStruct((8, 4, 144,...]
where the time goes in v2:
time: 153 us
  Pallas kernels  140 us (92%)
  local copies, waits for them, and re-layouts  12 us (8%)
    pallas_call x1, Pallas kernels, sum_over_devices(): pl.pallas_call(sum_kernel, out_shape=(jax.ShapeDtypeStruct((4, 32, WIDE),...  78.9 us
    pallas_call x1, Pallas kernels, attention(): pl.pallas_call(functools.partial(attention_kernel, cols - WINDOW, rows -...  19.9 us
    pallas_call x1, Pallas kernels, with_halo(): pl.pallas_call(halo_kernel, out_shape=jax.ShapeDtypeStruct((4, 384, 2 * I...  17 us
    pallas_call x1, Pallas kernels, returned(): pl.pallas_call(return_kernel, out_shape=jax.ShapeDtypeStruct((512, 2 * IN...  15.3 us
    unnamed x20, local copies, waits for them, and re-layouts  10.6 us
    pallas_call x1, Pallas kernels, weight_grads(): pl.pallas_call(weight_kernel, out_shape=jax.ShapeDtypeStruct((8, 4, 144,...  5 us
    pallas_call x1, Pallas kernels, project(): pl.pallas_call(project_kernel, out_shape=(jax.ShapeDtypeStruct((2, half,...  4.2 us

profile of v2, /device:TPU:1, one launch (start us, length us, event | category | flops | bytes accessed | tf_op | source)
XLA Modules:
  0.0 153.1 jit_solution(16929475590201537881)
XLA Ops:
  0.6 0.0 copy-start.1
  0.6 2.1 %copy-done.1 = bf16[1152,1728]{0,1:T(8,128)(2,1)S(1)} copy-done((bf16[1152,1728]{0,1:T(8,128)(2,1)S(1)}, bf16[1152,1728]{0,1:T(8,128)(2,1)}, u32[]{:S(2)}) %copy-start.1) | copy-done | bytes 3981336
  2.8 0.0 copy-start.3
  2.8 1.3 copy-done.3
  4.1 0.0 copy-start.5
  4.1 1.3 copy-done.5
  5.4 0.0 copy-start.7
  5.4 1.3 copy-done.7
  6.6 4.2 %project.1 = (bf16[2,256,640]{2,1,0:T(8,128)(2,1)S(1)}, bf16[2,256,1152]{2,1,0:T(8,128)(2,1)S(1)}, bf16[2,256,640]{2,1,0:T(8,128)(2,1)S(1)}) custom-call(bf16[512,1152]{1,0:T(8,128)(2,1)S(1)} %bitcast.20, bf16[512,1152]{1,0:T(8,128)(2,1)S(1)} %bitcast.22, bf16[1728,1152]{1,0:T(8,128)(2,1)S(1)} %bitcast.16, bf16[576,1152]{1,0:T(8,128)(2,1)S(1)} %bitcast.18), custom_call_target="tpu_custom_call" | custom-call | tf_op jit(solution)/shard_map/project/pallas_call | solution.py:58
  10.8 17.0 %halo.1.ext_ref = bf16[4,384,1152]{2,1,0:T(8,128)(2,1)S(1)} custom-call(bf16[2,256,1152]{2,1,0:T(8,128)(2,1)S(1)} %get-tuple-element.13.kv_ref), custom_call_target="tpu_custom_call" | custom-call | tf_op jit(solution)/shard_map/halo/pallas_call | solution.py:192
  27.8 19.9 %attention.1 = (bf16[512,640]{1,0:T(8,128)(2,1)S(1)}, bf16[512,640]{1,0:T(8,128)(2,1)S(1)}, bf16[4,384,1152]{2,1,0:T(8,128)(2,1)S(1)}) custom-call(bf16[4,384,1152]{2,1,0:T(8,128)(2,1)S(1)} %halo.1.ext_ref, bf16[2,256,640]{2,1,0:T(8,128)(2,1)S(1)} %get-tuple-element.14.q_ref, bf16[2,256,640]{2,1,0:T(8,128)(2,1)S(1)} %get-tuple-element.15.ga_ref), custom_call_target="tpu_custom_call" | custom-call | tf_op jit(solution)/shard_map/attention/pallas_call | solution.py:326
  47.7 0.0 copy-start.6
  47.7 0.0 copy-start.8
  47.7 15.3 %give_back.1.dkv_ref = bf16[512,1152]{1,0:T(8,128)(2,1)S(1)} custom-call(bf16[4,384,1152]{2,1,0:T(8,128)(2,1)S(1)} %get-tuple-element.17.dkv_ref), custom_call_target="tpu_custom_call" | custom-call | tf_op jit(solution)/shard_map/give_back/pallas_call | solution.py:443
  63.0 0.0 copy-done.6
  63.0 0.0 copy-done.8
  63.0 0.0 copy-start.2
  63.0 0.0 copy-start.4
  63.1 5.0 %weight_grads.1 = bf16[8,4,144,640]{3,2,1,0:T(8,128)(2,1)S(1)} custom-call(bf16[512,1152]{1,0:T(8,128)(2,1)S(1)} %bitcast.21, bf16[512,1152]{1,0:T(8,128)(2,1)S(1)} %bitcast.23, bf16[512,640]{1,0:T(8,128)(2,1)S(1)} %get-tuple-element.16.dq_ref, bf16[512,1152]{1,0:T(8,128)(2,1)S(1)} %give_back.1.dkv_ref, bf16[512,640]{1,0:T(8,128)(2,1)S(1)} %get-tuple-element.18.att_ref), custom_call_target="tpu_custom_call" | custom-call | tf_op jit(solution)/shard_map/weight_grads/pallas_call | solution.py:488
  68.1 0.0 copy-start
  68.1 2.5 %copy-done = bf16[8,4,144,640]{3,2,1,0:T(8,128)(2,1)} copy-done((bf16[8,4,144,640]{3,2,1,0:T(8,128)(2,1)}, bf16[8,4,144,640]{3,2,1,0:T(8,128)(2,1)S(1)}, u32[]{:S(2)}) %copy-start) | copy-done | bytes 5898264
  70.6 0.0 copy-done.2
  70.6 0.0 copy-done.4
  70.6 78.9 %sum_over_devices.1 = (bf16[4,32,640]{2,1,0:T(8,128)(2,1)S(1)}, bf16[512,1152]{1,0:T(8,128)(2,1)S(1)}, bf16[512,1152]{1,0:T(8,128)(2,1)S(1)}) custom-call(bf16[2,4,4,144,640]{4,3,2,1,0:T(8,128)(2,1)} %bitcast.15, bf16[512,640]{1,0:T(8,128)(2,1)S(1)} %get-tuple-element.16.dq_ref, bf16[512,1152]{1,0:T(8,128)(2,1)S(1)} %give_back.1.dkv_ref, ...), custom_call_target="tpu_custom_call" | custom-call | tf_op jit(solution)/shard_map/sum_over_devices/pallas_call | solution.py:706
  149.6 0.7 slice_bitcast_fusion
  150.3 0.8 concatenate.3
  151.0 1.0 copy.10
  152.0 1.0 copy.11
  (1 shorter events, 0.0 us)
Async XLA Ops:
  0.6 2.1 %copy-start.1 = (bf16[1152,1728]{0,1:T(8,128)(2,1)S(1)}, bf16[1152,1728]{0,1:T(8,128)(2,1)}, u32[]{:S(2)}) copy-start(bf16[1152,1728]{0,1:T(8,128)(2,1)} %param.5) | copy-start | bytes 11943940
  2.8 1.3 copy-start.3
  4.1 1.3 copy-start.5
  5.4 1.3 copy-start.7
  47.7 15.3 %copy-start.6 = (bf16[1,32,16,1152]{3,2,1,0:T(8,128)(2,1)S(1)}, bf16[1,32,16,1152]{3,2,1,0:T(8,128)(2,1)}, u32[]{:S(2)}) copy-start(bf16[1,32,16,1152]{3,2,1,0:T(8,128)(2,1)} %param.4) | copy-start | bytes 3538948
  47.7 15.3 %copy-start.8 = (bf16[1,32,16,1152]{3,2,1,0:T(8,128)(2,1)S(1)}, bf16[1,32,16,1152]{3,2,1,0:T(8,128)(2,1)}, u32[]{:S(2)}) copy-start(bf16[1,32,16,1152]{3,2,1,0:T(8,128)(2,1)} %param.7) | copy-start | bytes 3538948
  63.0 7.6 %copy-start.2 = (bf16[1152,1728]{0,1:T(8,128)(2,1)S(1)}, bf16[1152,1728]{0,1:T(8,128)(2,1)}, u32[]{:S(2)}) copy-start(bf16[1152,1728]{0,1:T(8,128)(2,1)} %param.5) | copy-start | bytes 11943940
  63.0 7.6 %copy-start.4 = (bf16[1152,576]{0,1:T(8,128)(2,1)S(1)}, bf16[1152,576]{0,1:T(8,128)(2,1)}, u32[]{:S(2)}) copy-start(bf16[1152,576]{0,1:T(8,128)(2,1)} %param.6) | copy-start | bytes 3981316
  68.1 2.5 %copy-start = (bf16[8,4,144,640]{3,2,1,0:T(8,128)(2,1)}, bf16[8,4,144,640]{3,2,1,0:T(8,128)(2,1)S(1)}, u32[]{:S(2)}) copy-start(bf16[8,4,144,640]{3,2,1,0:T(8,128)(2,1)S(1)} %weight_grads.1) | copy-start | bytes 17694724

commit v3 on v1

v3 whole, which is shorter than its diff:
```python
import functools

import jax
import jax.numpy as jnp
from jax import lax
from jax.experimental import pallas as pl
from jax.experimental.pallas import tpu as pltpu
from jax.sharding import PartitionSpec as P

H = 8
DH = 72
REACH = 8
WINDOW = 17
INNER = H * DH
PAIRS = H // 2
SPAN = 256
WIDE = 640
SHIFT = 64

masked_score = -1e30
bf16 = jnp.bfloat16
f32 = jnp.float32
MESH = pl.DeviceIdType.MESH
VMEM_SPEC = pl.BlockSpec(memory_space=pltpu.VMEM)
HBM_SPEC = pl.BlockSpec(memory_space=pltpu.HBM)


def mm(a, b):
    return jnp.dot(a, b, preferred_element_type=f32)


def mm_nt(a, b):
    return lax.dot_general(a, b, (((1,), (1,)), ((), ())), preferred_element_type=f32)


def by_column_block(rows):
    count, width = rows.shape
    parts = rows.reshape(count // 16, 2, 8, width)
    return [parts[:, j].reshape(count // 2, width) for j in range(2)]


CORNERS = [(dr, dc) for dr in (-1, 1) for dc in (-1, 1)]


def halo_part(dr, dc):
    blocks = {-1: slice(0, 1), 0: slice(1, 3), 1: slice(3, 4)}[dc]
    tokens = {-1: slice(0, 64), 0: slice(64, 320), 1: slice(320, 384)}[dr]
    return blocks, tokens


def size_of(part):
    return tuple(s.stop - s.start for s in part)


def place():
    return lax.axis_index("row"), lax.axis_index("col")


def inside(row, col):
    rows, cols = lax.axis_size("row"), lax.axis_size("col")
    return (row >= 0) & (row < rows) & (col >= 0) & (col < cols)


def remote(src, dst, send, recv, target):
    return pltpu.make_async_remote_copy(
        src_ref=src, dst_ref=dst, send_sem=send, recv_sem=recv, device_id=target, device_id_type=MESH
    )


RELAYS = [(7, 0), (0, 1)]


def meets(row, col):
    ways = []
    for dr, dc in ((-1, 0), (1, 0), (0, -1), (0, 1)):
        across = ((row == 3) & (dr == 1)) | ((row == 4) & (dr == -1))
        ways.append((inside(row + dr, col + dc) & jnp.logical_not(across), row + dr, col + dc))
    at_relay = (row == 0) | (row == 7)
    at_edge = (row == 3) | (row == 4)
    for relay_row, edge_row in ((0, 3), (7, 4)):
        ways.append((at_relay | at_edge, jnp.where(at_relay, edge_row, relay_row), col))
    return ways


def greet(ways):
    barrier = pltpu.get_barrier_semaphore()
    count = jnp.int32(0)
    for there, row, col in ways:
        count = count + there.astype(jnp.int32)

        @pl.when(there)
        def _():
            pl.semaphore_signal(
                barrier, inc=1, device_id={"row": row, "col": col}, device_id_type=MESH
            )

    return barrier, count


class RowExchange:
    def __init__(self, row, col, src, dst, relay, send, recv, relay_send, relay_recv):
        self.row, self.col = row, col
        self.src, self.dst, self.relay = src, dst, relay
        self.send_sem, self.recv_sem = send, recv
        self.relay_send, self.relay_recv = relay_send, relay_recv

    def has(self, k):
        return inside(self.row + 2 * k - 1, self.col)

    def across(self, k):
        return self.row == (3 if k == 1 else 4)

    def direct(self, k, cb):
        target = {"row": self.row + 2 * k - 1, "col": self.col}
        return remote(
            self.src(k, cb), self.dst(k, cb), self.send_sem.at[k, cb], self.recv_sem.at[k, cb], target
        )

    def first(self, k, cb):
        target = {"row": RELAYS[cb][0], "col": self.col}
        return remote(
            self.src(k, cb), self.relay.at[k], self.send_sem.at[k, cb], self.relay_recv.at[k], target
        )

    def second(self, k, cb):
        target = {"row": 4 if k == 1 else 3, "col": self.col}
        return remote(
            self.relay.at[k], self.dst(k, cb), self.relay_send.at[k], self.recv_sem.at[k, cb], target
        )

    def start(self, k, cb):
        @pl.when(self.has(k) & jnp.logical_not(self.across(k)))
        def _():
            self.direct(k, cb).start()

        @pl.when(self.across(k))
        def _():
            self.first(k, cb).start()

    def pass_on(self):
        for relay_row, cb in RELAYS:

            @pl.when(self.row == relay_row)
            def _():
                for k in range(2):
                    self.first(k, cb).wait_recv()
                    self.second(k, cb).start()

    def wait_recv(self, k, cb):
        self.direct(k, cb).wait_recv()

    def wait_sends(self):
        for k in range(2):

            @pl.when(self.has(k))
            def _():
                for cb in range(2):
                    self.direct(k, cb).wait_send()

        for relay_row, cb in RELAYS:

            @pl.when(self.row == relay_row)
            def _():
                for k in range(2):
                    self.second(k, cb).wait_send()


def head_kernel(
    tok_hbm, up_hbm, wqkv_hbm, wout_hbm, q_ref, ga_ref, ext_ref, tok, up, wqkv, wout, relay,
    load_sem, send_row, recv_row, relay_send, relay_recv, send_col, recv_col,
):
    row, col = place()
    loads = [
        pltpu.make_async_copy(src, dst, load_sem.at[n])
        for n, (src, dst) in enumerate(
            (
                (tok_hbm, tok),
                (wqkv_hbm.at[pl.ds(INNER, 2 * INNER)], wqkv.at[pl.ds(INNER, 2 * INNER)]),
                (wqkv_hbm.at[pl.ds(0, INNER)], wqkv.at[pl.ds(0, INNER)]),
                (up_hbm, up),
                (wout_hbm, wout),
            )
        )
    ]
    for load in loads:
        load.start()
    barrier, count = greet(meets(row, col))
    loads[0].wait()
    loads[1].wait()
    x = tok[...]
    key = by_column_block(mm_nt(x, wqkv[INNER : 2 * INNER]))
    value = by_column_block(mm_nt(x, wqkv[2 * INNER :]))
    for j in range(2):
        ext_ref[1 + j, 64:320] = jnp.concatenate([key[j], value[j]], axis=1).astype(bf16)
    pl.semaphore_wait(barrier, count)

    rows = RowExchange(
        row, col,
        lambda k, cb: ext_ref.at[1 + cb, pl.ds(64 if k == 0 else 256, 64)],
        lambda k, cb: ext_ref.at[1 + cb, pl.ds(320 if k == 0 else 0, 64)],
        relay, send_row, recv_row, relay_send, relay_recv,
    )

    def sideways(n, dc):
        tokens = pl.ds((0, 320, 64)[n], (64, 64, 256)[n])
        k = (dc + 1) // 2
        return remote(
            ext_ref.at[2 if dc == -1 else 1, tokens], ext_ref.at[0 if dc == -1 else 3, tokens],
            send_col.at[k, n], recv_col.at[k, n], {"row": row, "col": col - dc},
        )

    for k in range(2):
        for cb in range(2):
            rows.start(k, cb)
    for dc in (-1, 1):

        @pl.when(inside(row, col - dc))
        def _():
            sideways(2, dc).start()

    for dr in (-1, 0, 1):
        for dc in (-1, 0, 1):
            if dr != 0 or dc != 0:

                @pl.when(jnp.logical_not(inside(row + dr, col + dc)))
                def _():
                    part = halo_part(dr, dc)
                    ext_ref[part] = jnp.zeros(size_of(part) + (2 * INNER,), bf16)

    loads[2].wait()
    query = by_column_block(mm_nt(x, wqkv[:WIDE]))
    for j in range(2):
        q_ref[j] = query[j].astype(bf16)
    loads[3].wait()
    loads[4].wait()
    grads = by_column_block(mm_nt(up[...], wout[...]))
    for j in range(2):
        blank = jnp.zeros((grads[j].shape[0], SHIFT), f32)
        ga_ref[j] = jnp.concatenate([blank, grads[j]], axis=1).astype(bf16)

    rows.pass_on()

    for n in range(2):
        for cb, dc in ((1, -1), (0, 1)):

            @pl.when(inside(row + 2 * n - 1, col))
            def _():
                rows.wait_recv(1 - n, cb)

            @pl.when(inside(row + 2 * n - 1, col) & inside(row, col - dc))
            def _():
                sideways(n, dc).start()

    for dc in (-1, 1):

        @pl.when(inside(row, col + dc))
        def _():
            sideways(2, dc).wait_recv()

        @pl.when(inside(row, col - dc))
        def _():
            sideways(2, dc).wait_send()

        for n in range(2):

            @pl.when(inside(row + 2 * n - 1, col + dc))
            def _():
                sideways(n, dc).wait_recv()

            @pl.when(inside(row + 2 * n - 1, col) & inside(row, col - dc))
            def _():
                sideways(n, dc).wait_send()

    rows.wait_sends()


def head(token_rows, grad_rows, qkv_turned, out_turned):
    dma = pltpu.SemaphoreType.DMA
    half = token_rows.shape[0] // 2
    return pl.pallas_call(
        head_kernel,
        out_shape=(
            jax.ShapeDtypeStruct((2, half, WIDE), bf16),
            jax.ShapeDtypeStruct((2, half, WIDE), bf16),
            jax.ShapeDtypeStruct((4, 384, 2 * INNER), bf16),
        ),
        in_specs=[HBM_SPEC] * 4,
        out_specs=(VMEM_SPEC,) * 3,
        scratch_shapes=[
            pltpu.VMEM(token_rows.shape, bf16),
            pltpu.VMEM(token_rows.shape, bf16),
            pltpu.VMEM(qkv_turned.shape, bf16),
            pltpu.VMEM(out_turned.shape, bf16),
            pltpu.VMEM((2, 64, 2 * INNER), bf16),
            dma((5,)),
            dma((2, 2)),
            dma((2, 2)),
            dma((2,)),
            dma((2,)),
            dma((2, 3)),
            dma((2, 3)),
        ],
        compiler_params=pltpu.CompilerParams(
            collective_id=0, has_side_effects=True, vmem_limit_bytes=32 * 2**20
        ),
        name="head",
    )(token_rows, grad_rows, qkv_turned, out_turned)


def attention_kernel(
    cols_bound, rows_bound, ext_ref, q_ref, ga_ref, att_ref, dq_ref, dkv_ref,
    grads, k_turned, v_turned, bias, att_sum, dq_sum,
):
    row, col = place()
    row_first, col_first = row * 32, col * 16
    last_col = lax.axis_size("col") - 1
    exp_scale = DH ** (-0.5) * 1.4426950408889634

    for p in range(PAIRS):
        for cb in range(4):
            k_turned[p, cb] = ext_ref[cb, :, pl.ds(128 * p, SPAN)].T
            v_turned[p, cb] = ext_ref[cb, :, pl.ds(512 + 128 * p, SPAN)].T
    grads[...] = jnp.zeros_like(grads)
    att_sum[...] = jnp.zeros_like(att_sum)
    dq_sum[...] = jnp.zeros_like(dq_sum)

    at_row = lax.broadcasted_iota(jnp.int32, (SPAN, 128), 0)
    at_lane = lax.broadcasted_iota(jnp.int32, (128, SPAN), 1)

    def head_of(at, first):
        return (at >= first) & (at < first + DH)

    def split_turned(block, first):
        turned = block.T
        none = jnp.zeros_like(turned)
        return jnp.concatenate(
            [jnp.where(head_of(at_row, first + n * DH), turned, none) for n in range(2)], axis=1
        )

    def split_rows(block, first):
        none = jnp.zeros_like(block)
        return jnp.concatenate(
            [jnp.where(head_of(at_lane, first + n * DH), block, none) for n in range(2)], axis=0
        )

    def joined(turned, first):
        kept = jnp.where(
            head_of(at_row, first),
            turned[:, :128],
            jnp.where(head_of(at_row, first + DH), turned[:, 128:], 0.0),
        )
        return kept.T.reshape(16, 8, SPAN)

    def strip(s, _):
        j, t = s // 2, s % 2
        first_cb = jnp.where(col == 0, 1, jnp.where(col == last_col, 0, j))
        at = pl.multiple_of(128 * t, 128)
        band = pl.ds(at, 256)
        key_at = lax.broadcasted_iota(jnp.int32, (256, 128), 0)
        query_at = lax.broadcasted_iota(jnp.int32, (256, 128), 1)
        query_row = row_first + 16 * t + query_at // 8
        query_col = col_first + 8 * j + query_at % 8
        row_start = jnp.clip(query_row - REACH, 0, rows_bound)
        col_start = jnp.clip(query_col - REACH, 0, cols_bound)
        for b in range(3):
            key_row = row_first + 16 * t - REACH + key_at // 8
            key_col = col_first + 8 * (first_cb + b) - REACH + key_at % 8
            seen = (
                (key_row >= row_start)
                & (key_row <= row_start + 2 * REACH)
                & (key_col >= col_start)
                & (key_col <= col_start + 2 * REACH)
            )
            bias[b] = jnp.where(seen, 0.0, masked_score)
        for p in range(PAIRS):
            low, high = 16 * p, SHIFT + 16 * p
            here = pl.ds(128 * p, SPAN)
            there = pl.ds(512 + 128 * p, SPAN)
            query = q_ref[j, pl.ds(at, 128), here]
            upward = ga_ref[j, pl.ds(at, 128), here]
            query_turned = split_turned(query, low)
            upward_turned = split_turned(upward, high)
            scores = []
            for b in range(3):
                hidden = bias[b]
                scores.append(
                    mm(ext_ref[first_cb + b, band, here], query_turned)
                    + jnp.concatenate([hidden, hidden], axis=1)
                )
            top = functools.reduce(
                jnp.maximum, [jnp.max(x, axis=0, keepdims=True) for x in scores]
            )
            shifted = [jnp.exp2((x - top) * exp_scale) for x in scores]
            total = sum(jnp.sum(x, axis=0, keepdims=True) for x in shifted)
            inverse = 1.0 / total
            prob = [x * inverse for x in shifted]
            prob_low = [x.astype(bf16) for x in prob]
            dprob = [mm(ext_ref[first_cb + b, band, there], upward_turned) for b in range(3)]
            row_dot = sum(
                jnp.sum(x * y, axis=0, keepdims=True) for x, y in zip(prob, dprob)
            )
            dscore = [(x * (y - row_dot)).astype(bf16) for x, y in zip(prob, dprob)]
            att = sum(mm(v_turned[p, first_cb + b, :, band], prob_low[b]) for b in range(3))
            dquery = sum(mm(k_turned[p, first_cb + b, :, band], dscore[b]) for b in range(3))
            rows = pl.ds(16 * t, 16)
            att_sum[rows, j, :, here] += joined(att, high)
            dq_sum[rows, j, :, here] += joined(dquery, low)
            query_rows = split_rows(query, low)
            upward_rows = split_rows(upward, high)
            for b in range(3):
                grads[first_cb + b, band, here] += mm(dscore[b], query_rows)
                grads[first_cb + b, band, there] += mm(prob_low[b], upward_rows)
        return 0

    lax.fori_loop(0, 4, strip, 0)
    scale = DH ** (-0.5)
    att_ref[...] = att_sum[...].reshape(att_ref.shape).astype(bf16)
    dq_ref[...] = (dq_sum[...] * scale).reshape(dq_ref.shape).astype(bf16)
    for cb in range(4):
        dkv_ref[cb, :, :INNER] = (grads[cb, :, :INNER] * scale).astype(bf16)
        dkv_ref[cb, :, INNER:] = grads[cb, :, INNER:].astype(bf16)


def attention(ext, query, grad_att):
    rows = 32 * lax.axis_size("row")
    cols = 16 * lax.axis_size("col")
    tokens = 2 * query.shape[1]
    return pl.pallas_call(
        functools.partial(attention_kernel, cols - WINDOW, rows - WINDOW),
        out_shape=(
            jax.ShapeDtypeStruct((tokens, WIDE), bf16),
            jax.ShapeDtypeStruct((tokens, WIDE), bf16),
            jax.ShapeDtypeStruct(ext.shape, bf16),
        ),
        in_specs=[VMEM_SPEC] * 3,
        out_specs=(VMEM_SPEC,) * 3,
        scratch_shapes=[
            pltpu.VMEM(ext.shape, f32),
            pltpu.VMEM((PAIRS, 4, SPAN, 384), bf16),
            pltpu.VMEM((PAIRS, 4, SPAN, 384), bf16),
            pltpu.VMEM((3, 256, 128), f32),
            pltpu.VMEM((32, 2, 8, WIDE), f32),
            pltpu.VMEM((32, 2, 8, WIDE), f32),
        ],
        compiler_params=pltpu.CompilerParams(vmem_limit_bytes=36 * 2**20),
        name="attention",
    )(ext, query, grad_att)


PIECES = [(0, 64), (320, 64), (64, 256)]
UPPER = 64
LOWER = 144 - UPPER
EARLY = (0, 3)


def tail_kernel(
    dkv_ref, dq_ref, att_ref, tok_ref, up_ref, wqkv_ref, wout_ref,
    out_ref, tokens_grad_ref, sublayer_ref,
    side, up_down, flat, relay, total, dkv_own, dkv_pair, pair, pair_rows, turned,
    mine, rx1, ry1, a1, a2, rx2, ry2, b, rz, w, fin,
    send_col, recv_col, send_row, recv_row, relay_send, relay_recv, pair_sem,
    sem_x1, sem_y1, sem_x2, sem_y2, send_z, recv_z, send_f, recv_f, local_sem,
):
    img = lax.axis_index("img")
    row, col = place()
    z_hi, y = row // 4, row % 4
    z_lo, core = col // 2, col % 2
    z = z_hi * 4 + z_lo
    other = 1 - core

    def device(img=img, z_hi=z_hi, y=y, z_lo=z_lo, core=core):
        return {"img": img, "row": z_hi * 4 + y, "col": z_lo * 2 + core}

    barrier, count = greet(meets(row, col))
    greeted = [device(core=other)]
    greeted += [device(img=(img + d) % 4) for d in range(1, 4)]
    greeted += [device(img=(img + d) % 4, core=other) for d in range(1, 4)]
    greeted += [device(y=(y + d) % 4) for d in range(1, 4)]
    for d in range(1, 8):
        z_there = (z + d) % 8
        greeted.append(device(z_hi=z_there // 4, z_lo=z_there % 4))
    for target in greeted:
        pl.semaphore_signal(barrier, inc=1, device_id=target, device_id_type=MESH)
    pl.semaphore_wait(barrier, count + len(greeted))

    def to_side(k, piece):
        at = pl.ds(*PIECES[piece])
        return remote(
            dkv_ref.at[3 * k, at], side.at[k, at], send_col.at[k, piece], recv_col.at[k, piece],
            {"row": row, "col": col + 2 * k - 1},
        )

    def has_col(k):
        return inside(row, col + 2 * k - 1)

    def has_row(k):
        return inside(row + 2 * k - 1, col)

    for piece in range(3):
        for k in range(2):

            @pl.when(has_col(k))
            def _():
                to_side(k, piece).start()

    def to_pair(n, src, dst):
        return remote(src, dst, pair_sem.at[0, n], pair_sem.at[1, n], device(core=other))

    lanes_there = pl.ds(pl.multiple_of(512 * other, 128), WIDE)
    lanes_here = pl.ds(pl.multiple_of(512 * core, 128), WIDE)
    swaps = [
        to_pair(0, up_ref.at[:, lanes_there], pair_rows.at[1]),
        to_pair(1, att_ref, pair.at[1]),
        to_pair(2, tok_ref.at[:, lanes_there], pair_rows.at[0]),
        to_pair(3, dq_ref, pair.at[0]),
    ]
    for swap in swaps:
        swap.start()
    turned[0, :, :512] = tok_ref[:, lanes_here].T
    turned[1, :, :512] = up_ref[:, lanes_here].T

    rows = RowExchange(
        row, col, lambda k, cb: up_down.at[k, cb], lambda k, cb: flat.at[k, cb],
        relay, send_row, recv_row, relay_send, relay_recv,
    )

    def gather(piece, cb):
        at = pl.ds(*PIECES[piece])
        total[cb, at] = dkv_ref[1 + cb, at].astype(f32)

        @pl.when(has_col(cb))
        def _():
            to_side(1 - cb, piece).wait_recv()
            total[cb, at] += side[1 - cb, at].astype(f32)

    for k in range(2):
        for cb in range(2):

            @pl.when(has_row(k))
            def _():
                gather(k, cb)
                up_down[k, cb] = total[cb, pl.ds(*PIECES[k])].astype(bf16)

            rows.start(k, cb)

            @pl.when(jnp.logical_not(has_row(k)) & has_col(cb))
            def _():
                to_side(1 - cb, k).wait_recv()

    def weight_part(group, own, theirs):
        which = 1 if group == 3 else 0

        def part(n, _):
            at = pl.ds(pl.multiple_of(64 * core + 288 * n, 16), 288)
            grad = mm(turned[which, at, :512], own()) + mm(turned[which, at, 512:], theirs())
            mine[pl.ds(2 * n, 2), group] = grad.reshape(2, 144, WIDE).astype(bf16)
            return 0

        lax.fori_loop(0, 2, part, 0)

    swaps[0].wait_recv()
    turned[1, :, 512:] = pair_rows[1].T
    swaps[1].wait_recv()
    weight_part(3, lambda: att_ref[...], lambda: pair[1])
    swaps[2].wait_recv()
    turned[0, :, 512:] = pair_rows[0].T
    swaps[3].wait_recv()
    weight_part(0, lambda: dq_ref[...], lambda: pair[0])
    rows.pass_on()

    def over_x(d):
        x_there = (img + d) % 4
        return remote(
            mine.at[:, x_there, :UPPER], rx1.at[d - 1],
            sem_x1.at[0, d - 1], sem_x1.at[1, d - 1], device(img=x_there),
        )

    def over_y(d, group):
        y_there = (y + d) % 4
        return remote(
            mine.at[y_there, group, UPPER:], ry1.at[d - 1, group],
            sem_y1.at[0, d - 1, group], sem_y1.at[1, d - 1, group], device(y=y_there),
        )

    def send_first(groups):
        for d in range(1, 4):
            x_there = (img + d) % 4

            @pl.when((x_there == groups[0]) | (x_there == groups[1]))
            def _():
                over_x(d).start()

            for group in groups:
                over_y(d, group).start()

    send_first(EARLY)

    def outward(n, _):
        at = pl.ds(pl.multiple_of(256 * n, 256), 256)
        sublayer_ref[at] = mm(att_ref[at, SHIFT:], wout_ref[...]).astype(bf16)
        return 0

    lax.fori_loop(0, 2, outward, 0)
    gather(2, 0)
    gather(2, 1)
    for k in range(2):

        @pl.when(has_row(1 - k))
        def _():
            first = 64 if k == 1 else 256
            for cb in range(2):
                rows.wait_recv(k, cb)
                total[cb, pl.ds(first, 64)] += flat[k, cb].astype(f32)

    owned = total[:, 64:320].reshape(2, 32, 8, 2 * INNER)
    dkv_own[...] = jnp.stack([owned[0], owned[1]], axis=1).reshape(dkv_own.shape).astype(bf16)
    swaps.append(to_pair(4, dkv_own, dkv_pair))
    swaps[4].start()
    swaps[4].wait_recv()
    weight_part(1, lambda: dkv_own[:, :WIDE], lambda: dkv_pair[:, :WIDE])
    weight_part(
        2, lambda: dkv_own[:, 2 * INNER - WIDE :], lambda: dkv_pair[:, 2 * INNER - WIDE :]
    )
    send_first((1, 2))

    def inward(n, _):
        at = pl.ds(pl.multiple_of(256 * n, 256), 256)
        grad = mm(dq_ref[at, :INNER], wqkv_ref[:INNER]) + mm(dkv_own[at], wqkv_ref[INNER:])
        tokens_grad_ref[at] = grad.astype(bf16)
        return 0

    lax.fori_loop(0, 2, inward, 0)
    for d in range(1, 4):
        over_x(d).wait_recv()
        for group in range(4):
            over_y(d, group).wait_recv()

    def add_first(n, _):
        upper = mine[n, img, :UPPER].astype(f32)
        lower = mine[y, n, UPPER:].astype(f32)
        for d in range(3):
            upper += rx1[d, n].astype(f32)
            lower += ry1[d, n].astype(f32)
        a1[n] = upper.astype(bf16)
        a2[n] = lower.astype(bf16)
        return 0

    lax.fori_loop(0, 4, add_first, 0)

    second = []
    for d in range(1, 4):
        x_there, y_there = (img + d) % 4, (y + d) % 4
        second.append(
            remote(
                a1.at[y_there], ry2.at[d - 1],
                sem_y2.at[0, d - 1], sem_y2.at[1, d - 1], device(y=y_there),
            )
        )
        second.append(
            remote(
                a2.at[x_there], rx2.at[d - 1],
                sem_x2.at[0, d - 1], sem_x2.at[1, d - 1], device(img=x_there),
            )
        )
    for copy in second:
        copy.start()
    for copy in second:
        copy.wait_recv()
    upper = a1[y].astype(f32)
    lower = a2[img].astype(f32)
    for d in range(3):
        upper += ry2[d].astype(f32)
        lower += rx2[d].astype(f32)
    b[:UPPER] = upper.astype(bf16)
    b[UPPER:] = lower.astype(bf16)

    holder = z_hi == core

    def to_chip(n):
        return remote(
            b.at[pl.ds(32 * n, 48)], rz.at[z], send_z.at[n], recv_z.at[z],
            device(z_hi=core, z_lo=n),
        )

    def from_chip(n):
        return remote(
            b.at[pl.ds(0, 48)], rz.at[n], send_z.at[0], recv_z.at[n], device(core=other)
        )

    for n in range(4):

        @pl.when(jnp.logical_not(holder & (z_lo == n)))
        def _():
            to_chip(n).start()

    def to_owner(d, k):
        return remote(
            w.at[pl.ds(16 * k, 32)], fin.at[img], send_f.at[d, k], recv_f.at[img],
            device(img=(img + d) % 4, core=k),
        )

    @pl.when(holder)
    def _():
        for n in range(8):

            @pl.when(z != n)
            def _():
                from_chip(n).wait_recv()

        own = b[pl.ds(pl.multiple_of(32 * z_lo, 32), 48)].astype(f32)
        rz[z] = own.astype(bf16)
        added = rz[0].astype(f32)
        for n in range(1, 8):
            added += rz[n].astype(f32)
        w[...] = added.astype(bf16)
        for d in range(4):
            for k in range(2):

                @pl.when((core != k) | (d != 0))
                def _():
                    to_owner(d, k).start()

        kept = pltpu.make_async_copy(
            w.at[pl.ds(pl.multiple_of(16 * core, 16), 32)], fin.at[img], local_sem.at[4]
        )
        kept.start()
        kept.wait()

    def from_holder(n):
        return remote(
            w.at[pl.ds(0, 32)], fin.at[n], send_f.at[0, 0], recv_f.at[n], device(core=other)
        )

    for n in range(4):

        @pl.when(jnp.logical_not(holder) | (img != n))
        def _():
            from_holder(n).wait_recv()

    out_ref[...] = fin[...]

    rows.wait_sends()
    for k in range(2):

        @pl.when(has_col(k))
        def _():
            for piece in range(3):
                to_side(k, piece).wait_send()

    for d in range(1, 4):
        over_x(d).wait_send()
        for group in range(4):
            over_y(d, group).wait_send()
    for copy in swaps + second:
        copy.wait_send()
    for n in range(4):

        @pl.when(jnp.logical_not(holder & (z_lo == n)))
        def _():
            to_chip(n).wait_send()

    @pl.when(holder)
    def _():
        for d in range(4):
            for k in range(2):

                @pl.when((core != k) | (d != 0))
                def _():
                    to_owner(d, k).wait_send()


def tail(dkv, dq, att, token_rows, grad_rows, qkv_turned, out_turned):
    dma = pltpu.SemaphoreType.DMA
    tokens, width = token_rows.shape
    return pl.pallas_call(
        tail_kernel,
        out_shape=(
            jax.ShapeDtypeStruct((4, 32, WIDE), bf16),
            jax.ShapeDtypeStruct(token_rows.shape, bf16),
            jax.ShapeDtypeStruct(token_rows.shape, bf16),
        ),
        in_specs=[VMEM_SPEC] * 7,
        out_specs=(VMEM_SPEC,) * 3,
        scratch_shapes=[
            pltpu.VMEM((2, 384, 2 * INNER), bf16),
            pltpu.VMEM((2, 2, 64, 2 * INNER), bf16),
            pltpu.VMEM((2, 2, 64, 2 * INNER), bf16),
            pltpu.VMEM((2, 64, 2 * INNER), bf16),
            pltpu.VMEM((2, 384, 2 * INNER), f32),
            pltpu.VMEM((tokens, 2 * INNER), bf16),
            pltpu.VMEM((tokens, 2 * INNER), bf16),
            pltpu.VMEM((2, tokens, WIDE), bf16),
            pltpu.VMEM((2, tokens, WIDE), bf16),
            pltpu.VMEM((2, WIDE, 2 * tokens), bf16),
            pltpu.VMEM((4, 4, 144, WIDE), bf16),
            pltpu.VMEM((3, 4, UPPER, WIDE), bf16),
            pltpu.VMEM((3, 4, LOWER, WIDE), bf16),
            pltpu.VMEM((4, UPPER, WIDE), bf16),
            pltpu.VMEM((4, LOWER, WIDE), bf16),
            pltpu.VMEM((3, LOWER, WIDE), bf16),
            pltpu.VMEM((3, UPPER, WIDE), bf16),
            pltpu.VMEM((144, WIDE), bf16),
            pltpu.VMEM((8, 48, WIDE), bf16),
            pltpu.VMEM((48, WIDE), bf16),
            pltpu.VMEM((4, 32, WIDE), bf16),
            dma((2, 3)),
            dma((2, 3)),
            dma((2, 2)),
            dma((2, 2)),
            dma((2,)),
            dma((2,)),
            dma((2, 5)),
            dma((2, 3)),
            dma((2, 3, 4)),
            dma((2, 3)),
            dma((2, 3)),
            dma((4,)),
            dma((8,)),
            dma((4, 2)),
            dma((4,)),
            dma((5,)),
        ],
        compiler_params=pltpu.CompilerParams(
            collective_id=1, has_side_effects=True, vmem_limit_bytes=48 * 2**20
        ),
        name="tail",
    )(dkv, dq, att, token_rows, grad_rows, qkv_turned, out_turned)


def local(tokens, qkv_weight, out_weight, upstream):
    count = tokens.shape[1] * tokens.shape[2]
    width = tokens.shape[3]
    token_rows = tokens.reshape(count, width)
    grad_rows = upstream.reshape(count, width)
    qkv_turned, out_turned = qkv_weight.T, out_weight.T
    query, grad_att, extended = head(token_rows, grad_rows, qkv_turned, out_turned)
    att, dq, dkv = attention(extended, query, grad_att)
    shares, tokens_grad, sublayer_out = tail(
        dkv, dq, att, token_rows, grad_rows, qkv_turned, out_turned
    )
    shares = lax.dynamic_slice_in_dim(shares, 2 * lax.axis_index("col"), 18, 1).astype(f32)
    qkv_grad = jnp.concatenate(
        [shares[0, :, :INNER], shares[1, :, :INNER], shares[2, :, SHIFT:]], axis=1
    )
    return (
        sublayer_out.reshape(tokens.shape),
        tokens_grad.reshape(tokens.shape),
        qkv_grad,
        shares[3, :, SHIFT:],
    )


def solution(mesh):
    return jax.shard_map(
        local,
        mesh=mesh,
        in_specs=(P("img", "row", "col", None), P(), P(), P("img", "row", "col", None)),
        out_specs=(
            P("img", "row", "col", None),
            P("img", "row", "col", None),
            P(("row", "col"), None),
            P(("row", "col"), None),
        ),
        check_vma=False,
    )
```

time: 199 us -> 136 us (0.68)
  Pallas kernels: 170 us -> 124 us
  matrix products: 8.09 us -> 0 us
  local copies, waits for them, and re-layouts: 19.2 us -> 11.2 us
    pallas_call x5 -> x2, Pallas kernels: 146 us -> 104 us  [the longest x1 76.6 us: tail(): pl.pallas_call(tail_kernel, out_shape=(jax.ShapeDtypeStruct((4, 32, WIDE)...]
    dot_general x2 -> x0, matrix products: 8.09 us -> none  [the longest x1 5.86 us: local(): lax.dot_general(dqkv, qkv_weight, nt, preferred_element_type=f32)]
    unnamed x26 -> x16, local copies, waits for them, and re-layouts: 17.8 us -> 9.77 us
    pallas_call x1, Pallas kernels: 24 us -> 19.9 us  [attention(): pl.pallas_call(functools.partial(attention_kernel, cols - WINDOW, rows -...]
where the time goes in v3:
time: 136 us
  Pallas kernels  124 us (91%)
  local copies, waits for them, and re-layouts  11.2 us (8%)
    pallas_call x1, Pallas kernels, tail(): pl.pallas_call(tail_kernel, out_shape=(jax.ShapeDtypeStruct((4, 32, WIDE)...  76.6 us
    pallas_call x1, Pallas kernels, head(): pl.pallas_call(head_kernel, out_shape=(jax.ShapeDtypeStruct((2, half, WID...  27.7 us
    pallas_call x1, Pallas kernels, attention(): pl.pallas_call(functools.partial(attention_kernel, cols - WINDOW, rows -...  19.9 us
    unnamed x16, local copies, waits for them, and re-layouts  9.77 us

profile of v3, /device:TPU:1, one launch (start us, length us, event | category | flops | bytes accessed | tf_op | source)
XLA Modules:
  0.0 136.1 jit_solution(15495983523517030768)
XLA Ops:
  0.6 0.0 copy-start
  0.6 2.1 %copy-done = bf16[1152,1728]{0,1:T(8,128)(2,1)S(1)} copy-done((bf16[1152,1728]{0,1:T(8,128)(2,1)S(1)}, bf16[1152,1728]{0,1:T(8,128)(2,1)}, u32[]{:S(2)}) %copy-start) | copy-done | bytes 3981336
  2.8 0.0 copy-start.1
  2.8 1.3 copy-done.1
  4.1 0.0 copy-start.2
  4.1 1.3 copy-done.2
  5.4 0.0 copy-start.4
  5.4 1.3 copy-done.4
  6.6 27.7 %head.1 = (bf16[2,256,640]{2,1,0:T(8,128)(2,1)S(1)}, bf16[2,256,640]{2,1,0:T(8,128)(2,1)S(1)}, bf16[4,384,1152]{2,1,0:T(8,128)(2,1)S(1)}) custom-call(bf16[512,1152]{1,0:T(8,128)(2,1)S(1)} %bitcast.18, bf16[512,1152]{1,0:T(8,128)(2,1)S(1)} %bitcast.20, bf16[1728,1152]{1,0:T(8,128)(2,1)S(1)} %bitcast.15, bf16[576,1152]{1,0:T(8,128)(2,1)S(1)} %bitcast.17), custom_call_target="tpu_custom_call" | custom-call | tf_op jit(solution)/shard_map/head/pallas_call | solution.py:280
  34.3 0.0 copy-start.3
  34.4 0.0 copy-start.5
  34.4 19.9 %attention.1 = (bf16[512,640]{1,0:T(8,128)(2,1)S(1)}, bf16[512,640]{1,0:T(8,128)(2,1)S(1)}, bf16[4,384,1152]{2,1,0:T(8,128)(2,1)S(1)}) custom-call(bf16[4,384,1152]{2,1,0:T(8,128)(2,1)S(1)} %get-tuple-element.13.ext_ref, bf16[2,256,640]{2,1,0:T(8,128)(2,1)S(1)} %get-tuple-element.14.q_ref, bf16[2,256,640]{2,1,0:T(8,128)(2,1)S(1)} %get-tuple-element.15.ga_ref), custom_call_target="tpu_custom_call" | custom-call | tf_op jit(solution)/shard_map/attention/pallas_call | solution.py:428
  54.3 0.0 copy-start.6
  54.3 1.7 %copy-done.6 = bf16[4,384,1152]{2,1,0:T(8,128)(2,1)} copy-done((bf16[4,384,1152]{2,1,0:T(8,128)(2,1)}, bf16[4,384,1152]{2,1,0:T(8,128)(2,1)S(1)}, u32[]{:S(2)}) %copy-start.6) | copy-done | bytes 3538968
  56.0 0.0 copy-done.3
  56.0 0.0 copy-done.5
  56.0 76.6 %tail.1 = (bf16[4,32,640]{2,1,0:T(8,128)(2,1)S(1)}, bf16[512,1152]{1,0:T(8,128)(2,1)S(1)}, bf16[512,1152]{1,0:T(8,128)(2,1)S(1)}) custom-call(bf16[4,384,1152]{2,1,0:T(8,128)(2,1)} %copy-done.6, bf16[512,640]{1,0:T(8,128)(2,1)S(1)} %get-tuple-element.17.dq_ref, bf16[512,640]{1,0:T(8,128)(2,1)S(1)} %get-tuple-element.18.att_ref, ...), custom_call_target="tpu_custom_call" | custom-call | tf_op jit(solution)/shard_map/tail/pallas_call | solution.py:775
  132.6 0.7 slice_bitcast_fusion
  133.3 0.8 concatenate.3
  134.1 1.0 copy.10
  135.1 1.0 copy.11
  (1 shorter events, 0.0 us)
Async XLA Ops:
  0.6 2.1 %copy-start = (bf16[1152,1728]{0,1:T(8,128)(2,1)S(1)}, bf16[1152,1728]{0,1:T(8,128)(2,1)}, u32[]{:S(2)}) copy-start(bf16[1152,1728]{0,1:T(8,128)(2,1)} %param.5) | copy-start | bytes 11943940
  2.8 1.3 copy-start.1
  4.1 1.3 copy-start.2
  5.4 1.3 copy-start.4
  34.3 21.7 %copy-start.3 = (bf16[1,32,16,1152]{3,2,1,0:T(8,128)(2,1)S(1)}, bf16[1,32,16,1152]{3,2,1,0:T(8,128)(2,1)}, u32[]{:S(2)}) copy-start(bf16[1,32,16,1152]{3,2,1,0:T(8,128)(2,1)} %param.4) | copy-start | bytes 3538948
  34.4 21.7 %copy-start.5 = (bf16[1,32,16,1152]{3,2,1,0:T(8,128)(2,1)S(1)}, bf16[1,32,16,1152]{3,2,1,0:T(8,128)(2,1)}, u32[]{:S(2)}) copy-start(bf16[1,32,16,1152]{3,2,1,0:T(8,128)(2,1)} %param.7) | copy-start | bytes 3538948
  54.3 1.8 %copy-start.6 = (bf16[4,384,1152]{2,1,0:T(8,128)(2,1)}, bf16[4,384,1152]{2,1,0:T(8,128)(2,1)S(1)}, u32[]{:S(2)}) copy-start(bf16[4,384,1152]{2,1,0:T(8,128)(2,1)S(1)} %get-tuple-element.16.dkv_ref) | copy-start | bytes 10616836

commit v4 on v3

--- a/solution.py
+++ b/solution.py
@@ -22,7 +22,7 @@
 f32 = jnp.float32
 MESH = pl.DeviceIdType.MESH
 VMEM_SPEC = pl.BlockSpec(memory_space=pltpu.VMEM)
-HBM_SPEC = pl.BlockSpec(memory_space=pltpu.HBM)
+ANY_SPEC = pl.BlockSpec(memory_space=pl.ANY)
 
 
 def mm(a, b):
@@ -165,8 +165,9 @@
                     self.second(k, cb).wait_send()
 
 
-def head_kernel(
-    tok_hbm, up_hbm, wqkv_hbm, wout_hbm, q_ref, ga_ref, ext_ref, tok, up, wqkv, wout, relay,
+def front_kernel(
+    cols_bound, rows_bound, tok_hbm, up_hbm, wqkv_hbm, wout_hbm, ext_ref, att_ref, dq_ref, dkv_ref,
+    tok, up, wqkv, wout, relay, kv_ext, query_all, upward_all, grads, k_turned, v_turned, bias, att_sum, dq_sum,
     load_sem, send_row, recv_row, relay_send, relay_recv, send_col, recv_col,
 ):
     row, col = place()
@@ -186,12 +187,9 @@
         load.start()
     barrier, count = greet(meets(row, col))
     loads[0].wait()
-    loads[1].wait()
-    x = tok[...]
-    key = by_column_block(mm_nt(x, wqkv[INNER : 2 * INNER]))
-    value = by_column_block(mm_nt(x, wqkv[2 * INNER :]))
+    blocks = by_column_block(tok[...].astype(f32))
     for j in range(2):
-        ext_ref[1 + j, 64:320] = jnp.concatenate([key[j], value[j]], axis=1).astype(bf16)
+        ext_ref[1 + j, 64:320] = blocks[j].astype(bf16)
     pl.semaphore_wait(barrier, count)
 
     rows = RowExchange(
@@ -227,29 +225,62 @@
                     part = halo_part(dr, dc)
                     ext_ref[part] = jnp.zeros(size_of(part) + (2 * INNER,), bf16)
 
+    grads[...] = jnp.zeros_like(grads)
+    att_sum[...] = jnp.zeros_like(att_sum)
+    dq_sum[...] = jnp.zeros_like(dq_sum)
+
+    loads[1].wait()
+    x = ext_ref[1:3, 64:320].reshape(512, 2 * INNER)
+    keyvals = mm_nt(x, wqkv[INNER:])
+    kv_ext[1:3, 64:320] = keyvals.astype(bf16).reshape(2, 256, 2 * INNER)
     loads[2].wait()
-    query = by_column_block(mm_nt(x, wqkv[:WIDE]))
-    for j in range(2):
-        q_ref[j] = query[j].astype(bf16)
+    query_all[...] = mm_nt(x, wqkv[:WIDE]).astype(bf16).reshape(query_all.shape)
     loads[3].wait()
     loads[4].wait()
-    grads = by_column_block(mm_nt(up[...], wout[...]))
+    upward_grads = by_column_block(mm_nt(up[...], wout[...]))
     for j in range(2):
-        blank = jnp.zeros((grads[j].shape[0], SHIFT), f32)
-        ga_ref[j] = jnp.concatenate([blank, grads[j]], axis=1).astype(bf16)
+        blank = jnp.zeros((upward_grads[j].shape[0], SHIFT), f32)
+        upward_all[j] = jnp.concatenate([blank, upward_grads[j]], axis=1).astype(bf16)
+
+    def turn(chunk):
+        lanes = pl.ds(128 * chunk, 128)
+        for p in range(PAIRS):
+            for cb in range(4):
+                k_turned[p, cb, :, lanes] = kv_ext[cb, lanes, pl.ds(128 * p, SPAN)].T
+                v_turned[p, cb, :, lanes] = kv_ext[cb, lanes, pl.ds(512 + 128 * p, SPAN)].T
+
+    def pass_sideways(n):
+        for cb, dc in ((1, -1), (0, 1)):
+
+            @pl.when(inside(row + 2 * n - 1, col))
+            def _():
+                rows.wait_recv(1 - n, cb)
+
+            @pl.when(inside(row + 2 * n - 1, col) & inside(row, col - dc))
+            def _():
+                sideways(n, dc).start()
+
+    def finish_end(n):
+        for dc in (-1, 1):
+
+            @pl.when(inside(row + 2 * n - 1, col + dc))
+            def _():
+                sideways(n, dc).wait_recv()
+
+        at = pl.ds((0, 320)[n], 64)
+        ends = mm_nt(ext_ref[:, at].reshape(256, 2 * INNER), wqkv[INNER:])
+        kv_ext[:, at] = ends.astype(bf16).reshape(4, 64, 2 * INNER)
+        turn(2 * n)
+
+    def near(n):
+        return row != (4 if n == 0 else 3)
 
     rows.pass_on()
-
     for n in range(2):
-        for cb, dc in ((1, -1), (0, 1)):
-
-            @pl.when(inside(row + 2 * n - 1, col))
-            def _():
-                rows.wait_recv(1 - n, cb)
-
-            @pl.when(inside(row + 2 * n - 1, col) & inside(row, col - dc))
-            def _():
-                sideways(n, dc).start()
+
+        @pl.when(near(n))
+        def _():
+            pass_sideways(n)
 
     for dc in (-1, 1):
 
@@ -257,72 +288,25 @@
         def _():
             sideways(2, dc).wait_recv()
 
-        @pl.when(inside(row, col - dc))
-        def _():
-            sideways(2, dc).wait_send()
-
-        for n in range(2):
-
-            @pl.when(inside(row + 2 * n - 1, col + dc))
-            def _():
-                sideways(n, dc).wait_recv()
-
-            @pl.when(inside(row + 2 * n - 1, col) & inside(row, col - dc))
-            def _():
-                sideways(n, dc).wait_send()
-
-    rows.wait_sends()
-
-
-def head(token_rows, grad_rows, qkv_turned, out_turned):
-    dma = pltpu.SemaphoreType.DMA
-    half = token_rows.shape[0] // 2
-    return pl.pallas_call(
-        head_kernel,
-        out_shape=(
-            jax.ShapeDtypeStruct((2, half, WIDE), bf16),
-            jax.ShapeDtypeStruct((2, half, WIDE), bf16),
-            jax.ShapeDtypeStruct((4, 384, 2 * INNER), bf16),
-        ),
-        in_specs=[HBM_SPEC] * 4,
-        out_specs=(VMEM_SPEC,) * 3,
-        scratch_shapes=[
-            pltpu.VMEM(token_rows.shape, bf16),
-            pltpu.VMEM(token_rows.shape, bf16),
-            pltpu.VMEM(qkv_turned.shape, bf16),
-            pltpu.VMEM(out_turned.shape, bf16),
-            pltpu.VMEM((2, 64, 2 * INNER), bf16),
-            dma((5,)),
-            dma((2, 2)),
-            dma((2, 2)),
-            dma((2,)),
-            dma((2,)),
-            dma((2, 3)),
-            dma((2, 3)),
-        ],
-        compiler_params=pltpu.CompilerParams(
-            collective_id=0, has_side_effects=True, vmem_limit_bytes=32 * 2**20
-        ),
-        name="head",
-    )(token_rows, grad_rows, qkv_turned, out_turned)
-
-
-def attention_kernel(
-    cols_bound, rows_bound, ext_ref, q_ref, ga_ref, att_ref, dq_ref, dkv_ref,
-    grads, k_turned, v_turned, bias, att_sum, dq_sum,
-):
-    row, col = place()
+    x = jnp.concatenate([ext_ref[0, 64:320], ext_ref[3, 64:320]], axis=0)
+    keyvals = mm_nt(x, wqkv[INNER:]).astype(bf16)
+    kv_ext[0, 64:320] = keyvals[:256]
+    kv_ext[3, 64:320] = keyvals[256:]
+    turn(1)
+    for n in range(2):
+
+        @pl.when(near(n))
+        def _():
+            finish_end(n)
+
+        @pl.when(jnp.logical_not(near(n)))
+        def _():
+            at = pl.ds((0, 320)[n], 64)
+            kv_ext[:, at] = jnp.zeros((4, 64, 2 * INNER), bf16)
+
     row_first, col_first = row * 32, col * 16
     last_col = lax.axis_size("col") - 1
     exp_scale = DH ** (-0.5) * 1.4426950408889634
-
-    for p in range(PAIRS):
-        for cb in range(4):
-            k_turned[p, cb] = ext_ref[cb, :, pl.ds(128 * p, SPAN)].T
-            v_turned[p, cb] = ext_ref[cb, :, pl.ds(512 + 128 * p, SPAN)].T
-    grads[...] = jnp.zeros_like(grads)
-    att_sum[...] = jnp.zeros_like(att_sum)
-    dq_sum[...] = jnp.zeros_like(dq_sum)
 
     at_row = lax.broadcasted_iota(jnp.int32, (SPAN, 128), 0)
     at_lane = lax.broadcasted_iota(jnp.int32, (128, SPAN), 1)
@@ -344,15 +328,26 @@
         )
 
     def joined(turned, first):
-        kept = jnp.where(
-            head_of(at_row, first),
-            turned[:, :128],
-            jnp.where(head_of(at_row, first + DH), turned[:, 128:], 0.0),
-        )
-        return kept.T.reshape(16, 8, SPAN)
+        parts = [turned[:DH, :128], turned[DH:, 128:]]
+        if first:
+            parts = [jnp.zeros((first, 128), f32)] + parts
+        if first + 2 * DH < SPAN:
+            parts = parts + [jnp.zeros((SPAN - first - 2 * DH, 128), f32)]
+        return jnp.concatenate(parts, axis=0).T.reshape(16, 8, SPAN)
 
     def strip(s, _):
-        j, t = s // 2, s % 2
+        j = s % 2
+        t = jnp.where(row == 4, 1 - s // 2, s // 2)
+        for n, edge_row in ((1, 3), (0, 4)):
+
+            @pl.when((s == 1) & (row == edge_row))
+            def _():
+                pass_sideways(n)
+
+            @pl.when((s == 2) & (row == edge_row))
+            def _():
+                finish_end(n)
+
         first_cb = jnp.where(col == 0, 1, jnp.where(col == last_col, 0, j))
         at = pl.multiple_of(128 * t, 128)
         band = pl.ds(at, 256)
@@ -372,19 +367,17 @@
                 & (key_col <= col_start + 2 * REACH)
             )
             bias[b] = jnp.where(seen, 0.0, masked_score)
-        for p in range(PAIRS):
+        def weigh(p):
             low, high = 16 * p, SHIFT + 16 * p
             here = pl.ds(128 * p, SPAN)
             there = pl.ds(512 + 128 * p, SPAN)
-            query = q_ref[j, pl.ds(at, 128), here]
-            upward = ga_ref[j, pl.ds(at, 128), here]
-            query_turned = split_turned(query, low)
-            upward_turned = split_turned(upward, high)
+            query_turned = split_turned(query_all[j, pl.ds(at, 128), here], low)
+            upward_turned = split_turned(upward_all[j, pl.ds(at, 128), here], high)
             scores = []
             for b in range(3):
                 hidden = bias[b]
                 scores.append(
-                    mm(ext_ref[first_cb + b, band, here], query_turned)
+                    mm(kv_ext[first_cb + b, band, here], query_turned)
                     + jnp.concatenate([hidden, hidden], axis=1)
                 )
             top = functools.reduce(
@@ -395,21 +388,33 @@
             inverse = 1.0 / total
             prob = [x * inverse for x in shifted]
             prob_low = [x.astype(bf16) for x in prob]
-            dprob = [mm(ext_ref[first_cb + b, band, there], upward_turned) for b in range(3)]
+            dprob = [mm(kv_ext[first_cb + b, band, there], upward_turned) for b in range(3)]
             row_dot = sum(
                 jnp.sum(x * y, axis=0, keepdims=True) for x, y in zip(prob, dprob)
             )
             dscore = [(x * (y - row_dot)).astype(bf16) for x, y in zip(prob, dprob)]
-            att = sum(mm(v_turned[p, first_cb + b, :, band], prob_low[b]) for b in range(3))
-            dquery = sum(mm(k_turned[p, first_cb + b, :, band], dscore[b]) for b in range(3))
+            return prob_low, dscore
+
+        def spread(p, prob_low, dscore):
+            low, high = 16 * p, SHIFT + 16 * p
+            here = pl.ds(128 * p, SPAN)
+            there = pl.ds(512 + 128 * p, SPAN)
+            att = sum(mm(v_turned[p, first_cb + b, high : high + 2 * DH, band], prob_low[b]) for b in range(3))
+            dquery = sum(mm(k_turned[p, first_cb + b, low : low + 2 * DH, band], dscore[b]) for b in range(3))
             rows = pl.ds(16 * t, 16)
             att_sum[rows, j, :, here] += joined(att, high)
             dq_sum[rows, j, :, here] += joined(dquery, low)
-            query_rows = split_rows(query, low)
-            upward_rows = split_rows(upward, high)
+            query_rows = split_rows(query_all[j, pl.ds(at, 128), here], low)
+            upward_rows = split_rows(upward_all[j, pl.ds(at, 128), here], high)
             for b in range(3):
                 grads[first_cb + b, band, here] += mm(dscore[b], query_rows)
                 grads[first_cb + b, band, there] += mm(prob_low[b], upward_rows)
+
+        ready = weigh(0)
+        for p in range(PAIRS):
+            later = weigh(p + 1) if p + 1 < PAIRS else None
+            spread(p, *ready)
+            ready = later
         return 0
 
     lax.fori_loop(0, 4, strip, 0)
@@ -420,45 +425,78 @@
         dkv_ref[cb, :, :INNER] = (grads[cb, :, :INNER] * scale).astype(bf16)
         dkv_ref[cb, :, INNER:] = grads[cb, :, INNER:].astype(bf16)
 
-
-def attention(ext, query, grad_att):
-    rows = 32 * lax.axis_size("row")
-    cols = 16 * lax.axis_size("col")
-    tokens = 2 * query.shape[1]
+    for dc in (-1, 1):
+
+        @pl.when(inside(row, col - dc))
+        def _():
+            sideways(2, dc).wait_send()
+
+        for n in range(2):
+
+            @pl.when(inside(row + 2 * n - 1, col) & inside(row, col - dc))
+            def _():
+                sideways(n, dc).wait_send()
+
+    rows.wait_sends()
+
+
+def front(token_rows, grad_rows, qkv_turned, out_turned):
+    dma = pltpu.SemaphoreType.DMA
+    frame_rows = 32 * lax.axis_size("row")
+    frame_cols = 16 * lax.axis_size("col")
+    tokens, width = token_rows.shape
+    extended = (4, 384, width)
     return pl.pallas_call(
-        functools.partial(attention_kernel, cols - WINDOW, rows - WINDOW),
+        functools.partial(front_kernel, frame_cols - WINDOW, frame_rows - WINDOW),
         out_shape=(
+            jax.ShapeDtypeStruct(extended, bf16),
             jax.ShapeDtypeStruct((tokens, WIDE), bf16),
             jax.ShapeDtypeStruct((tokens, WIDE), bf16),
-            jax.ShapeDtypeStruct(ext.shape, bf16),
+            jax.ShapeDtypeStruct(extended, bf16),
         ),
-        in_specs=[VMEM_SPEC] * 3,
-        out_specs=(VMEM_SPEC,) * 3,
+        in_specs=[ANY_SPEC] * 4,
+        out_specs=(VMEM_SPEC,) * 4,
         scratch_shapes=[
-            pltpu.VMEM(ext.shape, f32),
+            pltpu.VMEM(token_rows.shape, bf16),
+            pltpu.VMEM(token_rows.shape, bf16),
+            pltpu.VMEM(qkv_turned.shape, bf16),
+            pltpu.VMEM(out_turned.shape, bf16),
+            pltpu.VMEM((2, 64, 2 * INNER), bf16),
+            pltpu.VMEM(extended, bf16),
+            pltpu.VMEM((2, 256, WIDE), bf16),
+            pltpu.VMEM((2, 256, WIDE), bf16),
+            pltpu.VMEM(extended, f32),
             pltpu.VMEM((PAIRS, 4, SPAN, 384), bf16),
             pltpu.VMEM((PAIRS, 4, SPAN, 384), bf16),
             pltpu.VMEM((3, 256, 128), f32),
             pltpu.VMEM((32, 2, 8, WIDE), f32),
             pltpu.VMEM((32, 2, 8, WIDE), f32),
+            dma((5,)),
+            dma((2, 2)),
+            dma((2, 2)),
+            dma((2,)),
+            dma((2,)),
+            dma((2, 3)),
+            dma((2, 3)),
         ],
-        compiler_params=pltpu.CompilerParams(vmem_limit_bytes=36 * 2**20),
-        name="attention",
-    )(ext, query, grad_att)
+        compiler_params=pltpu.CompilerParams(
+            collective_id=0, has_side_effects=True, vmem_limit_bytes=51 * 2**20
+        ),
+        name="front",
+    )(token_rows, grad_rows, qkv_turned, out_turned)
 
 
 PIECES = [(0, 64), (320, 64), (64, 256)]
-UPPER = 64
+UPPER = 80
 LOWER = 144 - UPPER
-EARLY = (0, 3)
 
 
 def tail_kernel(
-    dkv_ref, dq_ref, att_ref, tok_ref, up_ref, wqkv_ref, wout_ref,
-    out_ref, tokens_grad_ref, sublayer_ref,
-    side, up_down, flat, relay, total, dkv_own, dkv_pair, pair, pair_rows, turned,
-    mine, rx1, ry1, a1, a2, rx2, ry2, b, rz, w, fin,
-    send_col, recv_col, send_row, recv_row, relay_send, relay_recv, pair_sem,
+    ext_ref, dkv_ref, dq_ref, att_ref, tok_hbm, up_hbm, wqkv_hbm, wout_hbm,
+    out_ref, tokens_grad_ref, sublayer_ref, tok_ref, up_ref, wqkv_ref, wout_ref,
+    side, up_down, flat, relay, total, dkv_own, turned, ext_turned,
+    mine, theirs, recv0, rx1, ry1, a1, a2, rx2, ry2, b, rz, w, fin,
+    load_sem, send_col, recv_col, send_row, recv_row, relay_send, relay_recv, sem0,
     sem_x1, sem_y1, sem_x2, sem_y2, send_z, recv_z, send_f, recv_f, local_sem,
 ):
     img = lax.axis_index("img")
@@ -471,6 +509,14 @@
     def device(img=img, z_hi=z_hi, y=y, z_lo=z_lo, core=core):
         return {"img": img, "row": z_hi * 4 + y, "col": z_lo * 2 + core}
 
+    loads = [
+        pltpu.make_async_copy(src, dst, load_sem.at[n])
+        for n, (src, dst) in enumerate(
+            ((up_hbm, up_ref), (tok_hbm, tok_ref), (wout_hbm, wout_ref), (wqkv_hbm, wqkv_ref))
+        )
+    ]
+    for load in loads:
+        load.start()
     barrier, count = greet(meets(row, col))
     greeted = [device(core=other)]
     greeted += [device(img=(img + d) % 4) for d in range(1, 4)]
@@ -503,22 +549,6 @@
             def _():
                 to_side(k, piece).start()
 
-    def to_pair(n, src, dst):
-        return remote(src, dst, pair_sem.at[0, n], pair_sem.at[1, n], device(core=other))
-
-    lanes_there = pl.ds(pl.multiple_of(512 * other, 128), WIDE)
-    lanes_here = pl.ds(pl.multiple_of(512 * core, 128), WIDE)
-    swaps = [
-        to_pair(0, up_ref.at[:, lanes_there], pair_rows.at[1]),
-        to_pair(1, att_ref, pair.at[1]),
-        to_pair(2, tok_ref.at[:, lanes_there], pair_rows.at[0]),
-        to_pair(3, dq_ref, pair.at[0]),
-    ]
-    for swap in swaps:
-        swap.start()
-    turned[0, :, :512] = tok_ref[:, lanes_here].T
-    turned[1, :, :512] = up_ref[:, lanes_here].T
-
     rows = RowExchange(
         row, col, lambda k, cb: up_down.at[k, cb], lambda k, cb: flat.at[k, cb],
         relay, send_row, recv_row, relay_send, relay_recv,
@@ -533,40 +563,56 @@
             to_side(1 - cb, piece).wait_recv()
             total[cb, at] += side[1 - cb, at].astype(f32)
 
-    for k in range(2):
-        for cb in range(2):
-
-            @pl.when(has_row(k))
-            def _():
-                gather(k, cb)
-                up_down[k, cb] = total[cb, pl.ds(*PIECES[k])].astype(bf16)
-
-            rows.start(k, cb)
-
-            @pl.when(jnp.logical_not(has_row(k)) & has_col(cb))
-            def _():
-                to_side(1 - cb, k).wait_recv()
-
-    def weight_part(group, own, theirs):
-        which = 1 if group == 3 else 0
-
+    def return_ends():
+        for k in range(2):
+            for cb in range(2):
+
+                @pl.when(has_row(k))
+                def _():
+                    gather(k, cb)
+                    up_down[k, cb] = total[cb, pl.ds(*PIECES[k])].astype(bf16)
+
+                rows.start(k, cb)
+
+                @pl.when(jnp.logical_not(has_row(k)) & has_col(cb))
+                def _():
+                    to_side(1 - cb, k).wait_recv()
+
+    def weight_rows(half, n, group):
+        at = pl.ds(pl.multiple_of(576 * half + 288 * n, 32), 288)
+        if group == 3:
+            grad = mm(turned[1, at], att_ref[...])
+        elif group == 0:
+            grad = mm(turned[0, at], dq_ref[...])
+        else:
+            lanes = pl.ds(0 if group == 1 else 2 * INNER - WIDE, WIDE)
+            grad = mm(ext_turned[at], dkv_ref[:, :, lanes].reshape(1536, WIDE))
+        return grad.reshape(2, 144, WIDE)
+
+    def swap(group):
+        return remote(
+            theirs.at[:, group], recv0.at[:, group], sem0.at[0, group], sem0.at[1, group],
+            device(core=other),
+        )
+
+    def for_pair(group):
         def part(n, _):
-            at = pl.ds(pl.multiple_of(64 * core + 288 * n, 16), 288)
-            grad = mm(turned[which, at, :512], own()) + mm(turned[which, at, 512:], theirs())
-            mine[pl.ds(2 * n, 2), group] = grad.reshape(2, 144, WIDE).astype(bf16)
+            theirs[pl.ds(2 * n, 2), group] = weight_rows(other, n, group).astype(bf16)
             return 0
 
         lax.fori_loop(0, 2, part, 0)
-
-    swaps[0].wait_recv()
-    turned[1, :, 512:] = pair_rows[1].T
-    swaps[1].wait_recv()
-    weight_part(3, lambda: att_ref[...], lambda: pair[1])
-    swaps[2].wait_recv()
-    turned[0, :, 512:] = pair_rows[0].T
-    swaps[3].wait_recv()
-    weight_part(0, lambda: dq_ref[...], lambda: pair[0])
-    rows.pass_on()
+        swap(group).start()
+
+    def for_self(group):
+        swap(group).wait_recv()
+
+        def part(n, _):
+            at = pl.ds(2 * n, 2)
+            grad = weight_rows(core, n, group) + recv0[at, group].astype(f32)
+            mine[at, group] = grad.astype(bf16)
+            return 0
+
+        lax.fori_loop(0, 2, part, 0)
 
     def over_x(d):
         x_there = (img + d) % 4
@@ -582,24 +628,42 @@
             sem_y1.at[0, d - 1, group], sem_y1.at[1, d - 1, group], device(y=y_there),
         )
 
-    def send_first(groups):
+    def send_first(group):
         for d in range(1, 4):
-            x_there = (img + d) % 4
-
-            @pl.when((x_there == groups[0]) | (x_there == groups[1]))
+
+            @pl.when((img + d) % 4 == group)
             def _():
                 over_x(d).start()
 
-            for group in groups:
-                over_y(d, group).start()
-
-    send_first(EARLY)
+            over_y(d, group).start()
+
+    loads[0].wait()
+    turned[1] = up_ref[...].T
+    for_pair(3)
+    return_ends()
+    loads[1].wait()
+    turned[0] = tok_ref[...].T
+    for_pair(0)
+    for cb in range(4):
+        ext_turned[:, pl.ds(384 * cb, 384)] = ext_ref[cb].T
+    for_pair(1)
+    for_self(3)
+    send_first(3)
+    for_pair(2)
+    for_self(0)
+    send_first(0)
+    for_self(1)
+    send_first(1)
+    for_self(2)
+    send_first(2)
+    rows.pass_on()
 
     def outward(n, _):
         at = pl.ds(pl.multiple_of(256 * n, 256), 256)
         sublayer_ref[at] = mm(att_ref[at, SHIFT:], wout_ref[...]).astype(bf16)
         return 0
 
+    loads[2].wait()
     lax.fori_loop(0, 2, outward, 0)
     gather(2, 0)
     gather(2, 1)
@@ -614,14 +678,6 @@
 
     owned = total[:, 64:320].reshape(2, 32, 8, 2 * INNER)
     dkv_own[...] = jnp.stack([owned[0], owned[1]], axis=1).reshape(dkv_own.shape).astype(bf16)
-    swaps.append(to_pair(4, dkv_own, dkv_pair))
-    swaps[4].start()
-    swaps[4].wait_recv()
-    weight_part(1, lambda: dkv_own[:, :WIDE], lambda: dkv_pair[:, :WIDE])
-    weight_part(
-        2, lambda: dkv_own[:, 2 * INNER - WIDE :], lambda: dkv_pair[:, 2 * INNER - WIDE :]
-    )
-    send_first((1, 2))
 
     def inward(n, _):
         at = pl.ds(pl.multiple_of(256 * n, 256), 256)
@@ -629,7 +685,6 @@
         tokens_grad_ref[at] = grad.astype(bf16)
         return 0
 
-    lax.fori_loop(0, 2, inward, 0)
     for d in range(1, 4):
         over_x(d).wait_recv()
         for group in range(4):
@@ -664,6 +719,8 @@
         )
     for copy in second:
         copy.start()
+    loads[3].wait()
+    lax.fori_loop(0, 2, inward, 0)
     for copy in second:
         copy.wait_recv()
     upper = a1[y].astype(f32)
@@ -751,7 +808,9 @@
         over_x(d).wait_send()
         for group in range(4):
             over_y(d, group).wait_send()
-    for copy in swaps + second:
+    for group in range(4):
+        swap(group).wait_send()
+    for copy in second:
         copy.wait_send()
     for n in range(4):
 
@@ -769,7 +828,7 @@
                     to_owner(d, k).wait_send()
 
 
-def tail(dkv, dq, att, token_rows, grad_rows, qkv_turned, out_turned):
+def tail(ext, dkv, dq, att, token_rows, grad_rows, qkv_turned, out_turned):
     dma = pltpu.SemaphoreType.DMA
     tokens, width = token_rows.shape
     return pl.pallas_call(
@@ -779,19 +838,23 @@
             jax.ShapeDtypeStruct(token_rows.shape, bf16),
             jax.ShapeDtypeStruct(token_rows.shape, bf16),
         ),
-        in_specs=[VMEM_SPEC] * 7,
+        in_specs=[VMEM_SPEC] * 4 + [ANY_SPEC] * 4,
         out_specs=(VMEM_SPEC,) * 3,
         scratch_shapes=[
+            pltpu.VMEM(token_rows.shape, bf16),
+            pltpu.VMEM(token_rows.shape, bf16),
+            pltpu.VMEM(qkv_turned.shape, bf16),
+            pltpu.VMEM(out_turned.shape, bf16),
             pltpu.VMEM((2, 384, 2 * INNER), bf16),
             pltpu.VMEM((2, 2, 64, 2 * INNER), bf16),
             pltpu.VMEM((2, 2, 64, 2 * INNER), bf16),
             pltpu.VMEM((2, 64, 2 * INNER), bf16),
             pltpu.VMEM((2, 384, 2 * INNER), f32),
             pltpu.VMEM((tokens, 2 * INNER), bf16),
-            pltpu.VMEM((tokens, 2 * INNER), bf16),
-            pltpu.VMEM((2, tokens, WIDE), bf16),
-            pltpu.VMEM((2, tokens, WIDE), bf16),
-            pltpu.VMEM((2, WIDE, 2 * tokens), bf16),
+            pltpu.VMEM((2, width, tokens), bf16),
+            pltpu.VMEM((width, 4 * 384), bf16),
+            pltpu.VMEM((4, 4, 144, WIDE), bf16),
+            pltpu.VMEM((4, 4, 144, WIDE), bf16),
             pltpu.VMEM((4, 4, 144, WIDE), bf16),
             pltpu.VMEM((3, 4, UPPER, WIDE), bf16),
             pltpu.VMEM((3, 4, LOWER, WIDE), bf16),
@@ -803,13 +866,14 @@
             pltpu.VMEM((8, 48, WIDE), bf16),
             pltpu.VMEM((48, WIDE), bf16),
             pltpu.VMEM((4, 32, WIDE), bf16),
+            dma((4,)),
             dma((2, 3)),
             dma((2, 3)),
             dma((2, 2)),
             dma((2, 2)),
             dma((2,)),
             dma((2,)),
-            dma((2, 5)),
+            dma((2, 4)),
             dma((2, 3)),
             dma((2, 3, 4)),
             dma((2, 3)),
@@ -821,10 +885,10 @@
             dma((5,)),
         ],
         compiler_params=pltpu.CompilerParams(
-            collective_id=1, has_side_effects=True, vmem_limit_bytes=48 * 2**20
+            collective_id=1, has_side_effects=True, vmem_limit_bytes=50 * 2**20
         ),
         name="tail",
-    )(dkv, dq, att, token_rows, grad_rows, qkv_turned, out_turned)
+    )(ext, dkv, dq, att, token_rows, grad_rows, qkv_turned, out_turned)
 
 
 def local(tokens, qkv_weight, out_weight, upstream):
@@ -833,10 +897,9 @@
     token_rows = tokens.reshape(count, width)
     grad_rows = upstream.reshape(count, width)
     qkv_turned, out_turned = qkv_weight.T, out_weight.T
-    query, grad_att, extended = head(token_rows, grad_rows, qkv_turned, out_turned)
-    att, dq, dkv = attention(extended, query, grad_att)
+    extended, att, dq, dkv = front(token_rows, grad_rows, qkv_turned, out_turned)
     shares, tokens_grad, sublayer_out = tail(
-        dkv, dq, att, token_rows, grad_rows, qkv_turned, out_turned
+        extended, dkv, dq, att, token_rows, grad_rows, qkv_turned, out_turned
     )
     shares = lax.dynamic_slice_in_dim(shares, 2 * lax.axis_index("col"), 18, 1).astype(f32)
     qkv_grad = jnp.concatenate(

time: 136 us -> 117 us (0.86)
  Pallas kernels: 124 us -> 111 us
  local copies, waits for them, and re-layouts: 11.2 us -> 4.75 us
    pallas_call x1, Pallas kernels: 76.6 us -> 64.5 us  [tail(): pl.pallas_call(tail_kernel, out_shape=(jax.ShapeDtypeStruct((4, 32, WIDE)...]
    unnamed x16 -> x4, local copies, waits for them, and re-layouts: 9.77 us -> 3.29 us
    pallas_call x2 -> x1, Pallas kernels: 47.6 us -> 46.7 us  [front(): pl.pallas_call(functools.partial(front_kernel, frame_cols - WINDOW, frame...]
where the time goes in v4:
time: 117 us
  Pallas kernels  111 us (95%)
  local copies, waits for them, and re-layouts  4.75 us (4%)
    pallas_call x1, Pallas kernels, tail(): pl.pallas_call(tail_kernel, out_shape=(jax.ShapeDtypeStruct((4, 32, WIDE)...  64.5 us
    pallas_call x1, Pallas kernels, front(): pl.pallas_call(functools.partial(front_kernel, frame_cols - WINDOW, frame...  46.7 us
    unnamed x4, local copies, waits for them, and re-layouts  3.29 us

profile of v4, /device:TPU:1, one launch (start us, length us, event | category | flops | bytes accessed | tf_op | source)
XLA Modules:
  0.0 116.6 jit_solution(7230848107229907131)
XLA Ops:
  0.6 0.0 copy-start
  0.6 1.3 %copy-done = bf16[1,32,16,1152]{3,2,1,0:T(8,128)(2,1)S(1)} copy-done((bf16[1,32,16,1152]{3,2,1,0:T(8,128)(2,1)S(1)}, bf16[1,32,16,1152]{3,2,1,0:T(8,128)(2,1)}, u32[]{:S(2)}) %copy-start) | copy-done | bytes 1179672
  1.9 46.7 %front.1 = (bf16[4,384,1152]{2,1,0:T(8,128)(2,1)}, bf16[512,640]{1,0:T(8,128)(2,1)S(1)}, bf16[512,640]{1,0:T(8,128)(2,1)S(1)}, bf16[4,384,1152]{2,1,0:T(8,128)(2,1)}) custom-call(bf16[512,1152]{1,0:T(8,128)(2,1)S(1)} %bitcast.15, bf16[512,1152]{1,0:T(8,128)(2,1)} %bitcast.22, bf16[1728,1152]{1,0:T(8,128)(2,1)} %bitcast.18, bf16[576,1152]{1,0:T(8,128)(2,1)} %bitcast.20), custom_call_target="tpu_custom_call" | custom-call | tf_op jit(solution)/shard_map/front/pallas_call | solution.py:449
  48.6 64.5 %tail.1 = (bf16[4,32,640]{2,1,0:T(8,128)(2,1)S(1)}, bf16[512,1152]{1,0:T(8,128)(2,1)S(1)}, bf16[512,1152]{1,0:T(8,128)(2,1)S(1)}) custom-call(bf16[4,384,1152]{2,1,0:T(8,128)(2,1)} %get-tuple-element.11.ext_ref, bf16[4,384,1152]{2,1,0:T(8,128)(2,1)} %get-tuple-element.12.dkv_ref, bf16[512,640]{1,0:T(8,128)(2,1)S(1)} %get-tuple-element.13.dq_ref, ...), custom_call_target="tpu_custom_call" | custom-call | tf_op jit(solution)/shard_map/tail/pallas_call | solution.py:834
  113.2 0.7 slice_bitcast_fusion
  113.9 0.8 concatenate.3
  114.6 1.0 copy.10
  115.6 1.0 copy.11
  (1 shorter events, 0.0 us)
Async XLA Ops:
  0.6 1.3 %copy-start = (bf16[1,32,16,1152]{3,2,1,0:T(8,128)(2,1)S(1)}, bf16[1,32,16,1152]{3,2,1,0:T(8,128)(2,1)}, u32[]{:S(2)}) copy-start(bf16[1,32,16,1152]{3,2,1,0:T(8,128)(2,1)} %param.4) | copy-start | bytes 3538948

commit v5 on v4

--- a/solution.py
+++ b/solution.py
@@ -137,14 +137,14 @@
         def _():
             self.first(k, cb).start()
 
-    def pass_on(self):
+    def pass_on(self, late):
         for relay_row, cb in RELAYS:
+            k = 1 - cb if late else cb
 
             @pl.when(self.row == relay_row)
             def _():
-                for k in range(2):
-                    self.first(k, cb).wait_recv()
-                    self.second(k, cb).start()
+                self.first(k, cb).wait_recv()
+                self.second(k, cb).start()
 
     def wait_recv(self, k, cb):
         self.direct(k, cb).wait_recv()
@@ -275,7 +275,7 @@
     def near(n):
         return row != (4 if n == 0 else 3)
 
-    rows.pass_on()
+    rows.pass_on(False)
     for n in range(2):
 
         @pl.when(near(n))
@@ -304,6 +304,7 @@
             at = pl.ds((0, 320)[n], 64)
             kv_ext[:, at] = jnp.zeros((4, 64, 2 * INNER), bf16)
 
+    rows.pass_on(True)
     row_first, col_first = row * 32, col * 16
     last_col = lax.axis_size("col") - 1
     exp_scale = DH ** (-0.5) * 1.4426950408889634
@@ -589,95 +590,69 @@
             grad = mm(ext_turned[at], dkv_ref[:, :, lanes].reshape(1536, WIDE))
         return grad.reshape(2, 144, WIDE)
 
-    def swap(group):
-        return remote(
-            theirs.at[:, group], recv0.at[:, group], sem0.at[0, group], sem0.at[1, group],
-            device(core=other),
-        )
-
-    def for_pair(group):
-        def part(n, _):
-            theirs[pl.ds(2 * n, 2), group] = weight_rows(other, n, group).astype(bf16)
-            return 0
-
-        lax.fori_loop(0, 2, part, 0)
-        swap(group).start()
-
-    def for_self(group):
-        swap(group).wait_recv()
-
-        def part(n, _):
-            at = pl.ds(2 * n, 2)
+    def swap(n):
+        at = pl.ds(2 * n, 2)
+        return remote(
+            theirs.at[at], recv0.at[at], sem0.at[0, n], sem0.at[1, n], device(core=other)
+        )
+
+    def for_pair(n):
+        for group in range(4):
+            theirs[2 * n : 2 * n + 2, group] = weight_rows(other, n, group).astype(bf16)
+        swap(n).start()
+
+    def for_self(n):
+        swap(n).wait_recv()
+        for group in range(4):
+            at = slice(2 * n, 2 * n + 2)
             grad = weight_rows(core, n, group) + recv0[at, group].astype(f32)
             mine[at, group] = grad.astype(bf16)
-            return 0
-
-        lax.fori_loop(0, 2, part, 0)
-
-    def over_x(d):
+
+    def over_x(d, n):
         x_there = (img + d) % 4
-        return remote(
-            mine.at[:, x_there, :UPPER], rx1.at[d - 1],
-            sem_x1.at[0, d - 1], sem_x1.at[1, d - 1], device(img=x_there),
-        )
-
-    def over_y(d, group):
+        at = pl.ds(2 * n, 2)
+        return remote(
+            mine.at[at, x_there, :UPPER], rx1.at[d - 1, at],
+            sem_x1.at[0, d - 1, n], sem_x1.at[1, d - 1, n], device(img=x_there),
+        )
+
+    def over_y(d):
         y_there = (y + d) % 4
         return remote(
-            mine.at[y_there, group, UPPER:], ry1.at[d - 1, group],
-            sem_y1.at[0, d - 1, group], sem_y1.at[1, d - 1, group], device(y=y_there),
-        )
-
-    def send_first(group):
+            mine.at[y_there, :, UPPER:], ry1.at[d - 1],
+            sem_y1.at[0, d - 1], sem_y1.at[1, d - 1], device(y=y_there),
+        )
+
+    def send_first(n):
         for d in range(1, 4):
-
-            @pl.when((img + d) % 4 == group)
-            def _():
-                over_x(d).start()
-
-            over_y(d, group).start()
-
-    loads[0].wait()
-    turned[1] = up_ref[...].T
-    for_pair(3)
-    return_ends()
-    loads[1].wait()
-    turned[0] = tok_ref[...].T
-    for_pair(0)
-    for cb in range(4):
-        ext_turned[:, pl.ds(384 * cb, 384)] = ext_ref[cb].T
-    for_pair(1)
-    for_self(3)
-    send_first(3)
-    for_pair(2)
-    for_self(0)
-    send_first(0)
-    for_self(1)
-    send_first(1)
-    for_self(2)
-    send_first(2)
-    rows.pass_on()
+            over_x(d, n).start()
+
+            @pl.when((y + d) % 4 // 2 == n)
+            def _():
+                over_y(d).start()
 
     def outward(n, _):
         at = pl.ds(pl.multiple_of(256 * n, 256), 256)
         sublayer_ref[at] = mm(att_ref[at, SHIFT:], wout_ref[...]).astype(bf16)
         return 0
 
+    loads[0].wait()
+    turned[1] = up_ref[...].T
+    loads[1].wait()
+    turned[0] = tok_ref[...].T
+    for cb in range(4):
+        ext_turned[:, pl.ds(384 * cb, 384)] = ext_ref[cb].T
+    for_pair(0)
+    return_ends()
+    for_self(0)
+    send_first(0)
+    for_pair(1)
+    rows.pass_on(False)
     loads[2].wait()
     lax.fori_loop(0, 2, outward, 0)
-    gather(2, 0)
-    gather(2, 1)
-    for k in range(2):
-
-        @pl.when(has_row(1 - k))
-        def _():
-            first = 64 if k == 1 else 256
-            for cb in range(2):
-                rows.wait_recv(k, cb)
-                total[cb, pl.ds(first, 64)] += flat[k, cb].astype(f32)
-
-    owned = total[:, 64:320].reshape(2, 32, 8, 2 * INNER)
-    dkv_own[...] = jnp.stack([owned[0], owned[1]], axis=1).reshape(dkv_own.shape).astype(bf16)
+    for_self(1)
+    send_first(1)
+    rows.pass_on(True)
 
     def inward(n, _):
         at = pl.ds(pl.multiple_of(256 * n, 256), 256)
@@ -686,9 +661,9 @@
         return 0
 
     for d in range(1, 4):
-        over_x(d).wait_recv()
-        for group in range(4):
-            over_y(d, group).wait_recv()
+        over_x(d, 0).wait_recv()
+        over_x(d, 1).wait_recv()
+        over_y(d).wait_recv()
 
     def add_first(n, _):
         upper = mine[n, img, :UPPER].astype(f32)
@@ -719,8 +694,8 @@
         )
     for copy in second:
         copy.start()
-    loads[3].wait()
-    lax.fori_loop(0, 2, inward, 0)
+    gather(2, 0)
+    gather(2, 1)
     for copy in second:
         copy.wait_recv()
     upper = a1[y].astype(f32)
@@ -750,6 +725,20 @@
         def _():
             to_chip(n).start()
 
+    for k in range(2):
+
+        @pl.when(has_row(1 - k))
+        def _():
+            first = 64 if k == 1 else 256
+            for cb in range(2):
+                rows.wait_recv(k, cb)
+                total[cb, pl.ds(first, 64)] += flat[k, cb].astype(f32)
+
+    owned = total[:, 64:320].reshape(2, 32, 8, 2 * INNER)
+    dkv_own[...] = jnp.stack([owned[0], owned[1]], axis=1).reshape(dkv_own.shape).astype(bf16)
+    loads[3].wait()
+    lax.fori_loop(0, 2, inward, 0)
+
     def to_owner(d, k):
         return remote(
             w.at[pl.ds(16 * k, 32)], fin.at[img], send_f.at[d, k], recv_f.at[img],
@@ -805,11 +794,11 @@
                 to_side(k, piece).wait_send()
 
     for d in range(1, 4):
-        over_x(d).wait_send()
-        for group in range(4):
-            over_y(d, group).wait_send()
-    for group in range(4):
-        swap(group).wait_send()
+        over_x(d, 0).wait_send()
+        over_x(d, 1).wait_send()
+        over_y(d).wait_send()
+    for n in range(2):
+        swap(n).wait_send()
     for copy in second:
         copy.wait_send()
     for n in range(4):
@@ -873,9 +862,9 @@
             dma((2, 2)),
             dma((2,)),
             dma((2,)),
-            dma((2, 4)),
+            dma((2, 2)),
+            dma((2, 3, 2)),
             dma((2, 3)),
-            dma((2, 3, 4)),
             dma((2, 3)),
             dma((2, 3)),
             dma((4,)),

time: 117 us -> 113 us (0.966)
  Pallas kernels: 111 us -> 108 us
    pallas_call x1, Pallas kernels: 64.5 us -> 62.5 us  [tail(): pl.pallas_call(tail_kernel, out_shape=(jax.ShapeDtypeStruct((4, 32, WIDE)...]
    pallas_call x1, Pallas kernels: 46.7 us -> 45.1 us  [front(): pl.pallas_call(functools.partial(front_kernel, frame_cols - WINDOW, frame...]
where the time goes in v5:
time: 113 us
  Pallas kernels  108 us (96%)
  local copies, waits for them, and re-layouts  4.75 us (4%)
    pallas_call x1, Pallas kernels, tail(): pl.pallas_call(tail_kernel, out_shape=(jax.ShapeDtypeStruct((4, 32, WIDE)...  62.5 us
    pallas_call x1, Pallas kernels, front(): pl.pallas_call(functools.partial(front_kernel, frame_cols - WINDOW, frame...  45.1 us
    unnamed x4, local copies, waits for them, and re-layouts  3.29 us

profile of v5, /device:TPU:1, one launch (start us, length us, event | category | flops | bytes accessed | tf_op | source)
XLA Modules:
  0.0 113.0 jit_solution(4406019176296295945)
XLA Ops:
  0.6 0.0 copy-start
  0.6 1.3 %copy-done = bf16[1,32,16,1152]{3,2,1,0:T(8,128)(2,1)S(1)} copy-done((bf16[1,32,16,1152]{3,2,1,0:T(8,128)(2,1)S(1)}, bf16[1,32,16,1152]{3,2,1,0:T(8,128)(2,1)}, u32[]{:S(2)}) %copy-start) | copy-done | bytes 1179672
  1.9 45.1 %front.1 = (bf16[4,384,1152]{2,1,0:T(8,128)(2,1)}, bf16[512,640]{1,0:T(8,128)(2,1)S(1)}, bf16[512,640]{1,0:T(8,128)(2,1)S(1)}, bf16[4,384,1152]{2,1,0:T(8,128)(2,1)}) custom-call(bf16[512,1152]{1,0:T(8,128)(2,1)S(1)} %bitcast.15, bf16[512,1152]{1,0:T(8,128)(2,1)} %bitcast.22, bf16[1728,1152]{1,0:T(8,128)(2,1)} %bitcast.18, bf16[576,1152]{1,0:T(8,128)(2,1)} %bitcast.20), custom_call_target="tpu_custom_call" | custom-call | tf_op jit(solution)/shard_map/front/pallas_call | solution.py:450
  47.0 62.5 %tail.1 = (bf16[4,32,640]{2,1,0:T(8,128)(2,1)S(1)}, bf16[512,1152]{1,0:T(8,128)(2,1)S(1)}, bf16[512,1152]{1,0:T(8,128)(2,1)S(1)}) custom-call(bf16[4,384,1152]{2,1,0:T(8,128)(2,1)} %get-tuple-element.11.ext_ref, bf16[4,384,1152]{2,1,0:T(8,128)(2,1)} %get-tuple-element.12.dkv_ref, bf16[512,640]{1,0:T(8,128)(2,1)S(1)} %get-tuple-element.13.dq_ref, ...), custom_call_target="tpu_custom_call" | custom-call | tf_op jit(solution)/shard_map/tail/pallas_call | solution.py:823
  109.5 0.7 slice_bitcast_fusion
  110.2 0.8 concatenate.3
  111.0 1.0 copy.10
  112.0 1.0 copy.11
  (1 shorter events, 0.0 us)
Async XLA Ops:
  0.6 1.3 %copy-start = (bf16[1,32,16,1152]{3,2,1,0:T(8,128)(2,1)S(1)}, bf16[1,32,16,1152]{3,2,1,0:T(8,128)(2,1)}, u32[]{:S(2)}) copy-start(bf16[1,32,16,1152]{3,2,1,0:T(8,128)(2,1)} %param.4) | copy-start | bytes 3538948
